TPU v7x, 128 devices: a whole 4x4x4 slice. The times are simulated.
128 devices in a mesh: dp: 8 (over x_hi, y), slab: 16 (over z, x_lo, core).
Axes of the slice: x: 4 (x_hi: 2, x_lo: 2; x = x_hi * 2 + x_lo), y: 4, z: 4, core: 2. Of those that a mesh axis runs over, the one named last changes fastest.
Arguments:
- field: bfloat16 [8, 64, 64, 4096], P('dp', None, 'slab'), may hold values from -6 to 6
- cotangent: bfloat16 [8, 64, 64, 4096], P('dp', None, 'slab'), may hold values from -6 to 6
- spectral: bfloat16 [2, 64, 64, 32768], P(None, None, None, ('slab', 'dp')), may hold values from -1.5 to 1.5
- skip: bfloat16 [64, 64], replicated, may hold values from -0.75 to 0.75
- bias: float32 [64], replicated, may hold values from -3 to 3
Outputs:
- output: bfloat16 [8, 64, 64, 4096], P('dp', None, 'slab')
- field_grad: bfloat16 [8, 64, 64, 4096], P('dp', None, 'slab')
- spectral_grad: bfloat16 [2, 64, 64, 32768], P(None, None, None, ('slab', 'dp'))
- skip_grad: float32 [64, 64], replicated
- bias_grad: float32 [64], replicated
All inputs are finite; a program needn't handle non-finite values.
Results may differ from a plain program's by a relative error of at most 0.015.
Values may be sent and summed in bfloat16 or wider, within the bound.
A program may use at most 192 MiB of HBM per device.

v0:
```python
import math

import jax
import jax.numpy as jnp
from jax import lax
from jax.sharding import PartitionSpec as P

N = 64
M = 32


def tables():
    places = jnp.arange(N, dtype=jnp.int32)
    frequency = jnp.arange(M, dtype=jnp.int32) - M // 2
    phases = jnp.mod(places[:, None] * frequency[None, :], N)
    angles = jnp.mod(phases[:, None, :, None] + phases[None, :, None, :], N).astype(jnp.float32) * (
        2.0 * math.pi / N
    )
    plane_table = (jnp.stack([jnp.cos(angles), -jnp.sin(angles)], axis=2) / N).reshape(
        N * N, 2, M * M
    )
    line_angle = phases.astype(jnp.float32) * (2.0 * math.pi / N)
    cosine = jnp.cos(line_angle) / math.sqrt(N)
    sine = jnp.sin(line_angle) / math.sqrt(N)
    line_table = jnp.stack([jnp.stack([cosine, -sine], 1), jnp.stack([sine, cosine], 1)], 0)
    return (plane_table.astype(jnp.bfloat16), line_table.astype(jnp.bfloat16))


def group_width(columns):
    return math.gcd(columns, max(1, 128 // M))


def expand_forward(line_table, width):
    unit = jnp.eye(width, dtype=jnp.bfloat16)
    wide = jnp.einsum("rxtk,ij->rxitjk", line_table, unit)
    return wide.reshape(2, N, width, 2, width * M)


def expand_inverse(line_table, width):
    unit = jnp.eye(width, dtype=jnp.bfloat16)
    wide = jnp.einsum("txrk,ji->txrjki", line_table, unit)
    return wide.reshape(2, N, 2, width * M, width)


def line_forward(pencils, line_table):
    columns = pencils.shape[-1]
    width = group_width(columns)
    table = expand_forward(line_table, width)
    shaped = pencils.reshape(pencils.shape[:-1] + (columns // width, width))
    modes = jnp.einsum(
        "rbcxoi,rxitn->tbcon", shaped, table, preferred_element_type=jnp.float32
    ).astype(jnp.bfloat16)
    return modes.reshape(2, pencils.shape[1], pencils.shape[2], -1)


def line_inverse(modes, line_table):
    columns = modes.shape[-1] // M
    width = group_width(columns)
    table = expand_inverse(line_table, width)
    shaped = modes.reshape(modes.shape[:3] + (columns // width, width * M))
    lines = jnp.einsum(
        "rbcon,txrni->tbcxoi", shaped, table, preferred_element_type=jnp.float32
    ).astype(jnp.bfloat16)
    return lines.reshape(2, modes.shape[1], modes.shape[2], N, columns)


def shards(field, cotangent, spectral, skip, bias):
    plane_table, line_table = tables()
    local_samples = field.shape[0]
    data_count = lax.axis_size("dp")
    all_samples = local_samples * data_count

    def to_spectrum(values):
        planes = jnp.einsum(
            "scxp,ptq->tscxq", values, plane_table, preferred_element_type=jnp.float32
        ).astype(jnp.bfloat16)
        pencils = lax.all_to_all(
            lax.all_to_all(planes, "slab", split_axis=4, concat_axis=3, tiled=True),
            "dp",
            split_axis=4,
            concat_axis=1,
            tiled=True,
        )
        return line_forward(pencils, line_table)

    def to_spatial(modes):
        lines = line_inverse(modes, line_table)
        planes = lax.all_to_all(
            lax.all_to_all(lines, "dp", split_axis=1, concat_axis=4, tiled=True),
            "slab",
            split_axis=3,
            concat_axis=4,
            tiled=True,
        )
        return jnp.einsum(
            "tscxq,ptq->scxp", planes, plane_table, preferred_element_type=jnp.float32
        )

    weight_re = spectral[0]
    weight_im = spectral[1]
    modes_in = to_spectrum(field)
    in_re = modes_in[0]
    in_im = modes_in[1]
    product = lambda left, right: jnp.einsum(
        "biq,ioq->boq", left, right, preferred_element_type=jnp.float32
    )
    mixed_re = product(in_re, weight_re) - product(in_im, weight_im)
    mixed_im = product(in_re, weight_im) + product(in_im, weight_re)
    mixed = jnp.stack([mixed_re, mixed_im]).astype(jnp.bfloat16)
    spectral_part = to_spatial(mixed)
    pre = (
        spectral_part
        + jnp.einsum("bixp,io->boxp", field, skip, preferred_element_type=jnp.float32)
        + bias[None, :, None, None]
    )
    activate = lambda values: jax.nn.gelu(values, approximate=True)
    pre_value, pullback = jax.vjp(activate, pre)
    output = pre_value.astype(jnp.bfloat16)
    pre_grad = pullback(cotangent.astype(jnp.float32))[0].astype(jnp.bfloat16)
    modes_grad = to_spectrum(pre_grad)
    grad_re = modes_grad[0]
    grad_im = modes_grad[1]
    adjoint = lambda left, right: jnp.einsum(
        "boq,ioq->biq", left, right, preferred_element_type=jnp.float32
    )
    back_re = adjoint(grad_re, weight_re) + adjoint(grad_im, weight_im)
    back_im = adjoint(grad_im, weight_re) - adjoint(grad_re, weight_im)
    back_modes = jnp.stack([back_re, back_im]).astype(jnp.bfloat16)
    outer = lambda left, right: jnp.einsum(
        "biq,boq->ioq", left, right, preferred_element_type=jnp.float32
    )
    spec_re = outer(in_re, grad_re) + outer(in_im, grad_im)
    spec_im = outer(in_re, grad_im) - outer(in_im, grad_re)
    spectral_grad = jnp.stack([spec_re, spec_im]).astype(jnp.bfloat16)
    skip_back = jnp.einsum("boxp,io->bixp", pre_grad, skip, preferred_element_type=jnp.float32)
    field_grad = (to_spatial(back_modes) + skip_back).astype(jnp.bfloat16)
    skip_part = jnp.einsum("bixp,boxp->io", field, pre_grad, preferred_element_type=jnp.float32)
    bias_part = jnp.sum(pre_grad, axis=(0, 2, 3), dtype=jnp.float32)
    skip_total, bias_total = lax.psum((skip_part, bias_part), ("dp", "slab"))
    factor = 1.0 / math.sqrt(all_samples * N * N * N)
    return (output, field_grad, spectral_grad, skip_total * factor, bias_total * factor)


def solution(mesh):
    return jax.shard_map(
        shards,
        mesh=mesh,
        in_specs=(
            P("dp", None, "slab", None),
            P("dp", None, "slab", None),
            P(None, None, None, ("slab", "dp")),
            P(),
            P(),
        ),
        out_specs=(
            P("dp", None, "slab", None),
            P("dp", None, "slab", None),
            P(None, None, None, ("slab", "dp")),
            P(),
            P(),
        ),
        check_vma=False,
    )
```

profile of v0, /device:TPU:1, one launch (start us, length us, event | category | flops | bytes accessed | tf_op | source)
XLA Modules:
  0.0 603.8 jit_solution(4540181063021214853)
XLA Ops:
  0.7 11.4 %broadcast_add_fusion = s32[64,64,32,32]{1,0,3,2:T(8,128)} fusion(s32[64,32]{0,1:T(8,128)S(1)} %add_select_fusion.1), kind=kLoop, calls=%fused_computation.17 | loop fusion | flops 4194304 | bytes 16785408 | tf_op jit(solution)/shard_map/add | solution.py:16
  12.1 27.9 %add.157 = s32[4096,1,1024]{0,2,1:T(8,128)} reshape(s32[64,64,32,32]{1,0,3,2:T(8,128)} %broadcast_add_fusion) | data formatting | bytes 33554432 | tf_op jit(solution)/shard_map/add | solution.py:16
  40.1 17.4 %copy.202 = s32[4096,1,1024]{2,0,1:T(8,128)} copy(s32[4096,1,1024]{0,2,1:T(8,128)} %add.157) | data formatting | bytes 33554432 | tf_op jit(solution)/shard_map/add | solution.py:16
  57.5 66.8 %fusion.51 = (f32[4096,1,1024]{2,0,1:T(8,128)S(1)}, f32[4096,1,1024]{2,0,1:T(8,128)S(1)}) fusion(s32[4096,1,1024]{2,0,1:T(8,128)} %copy.202), kind=kLoop, calls=%fused_computation.66 | loop fusion | flops 58720256 | bytes 50331648 | tf_op jit(solution)/shard_map/cos | solution.py:19
  124.3 8.4 %fusion = bf16[4096,2,1024]{2,0,1:T(8,128)(2,1)} fusion(f32[4096,1,1024]{2,0,1:T(8,128)S(1)} %get-tuple-element.35, f32[4096,1,1024]{2,0,1:T(8,128)S(1)} %get-tuple-element.34), kind=kLoop, calls=%fused_computation.1 | loop fusion | flops 25165824 | bytes 50331648 | tf_op jit(solution)/shard_map/convert_element_type | solution.py:26
  132.8 8.6 %fusion.90 = bf16[2,1,64,4,1024]{4,2,3,0,1:T(8,128)(2,1)S(1)} fusion(bf16[64,4,4096]{2,1,0:T(4,128)(2,1)S(1)} %bitcast.370, bf16[4096,2,1024]{2,0,1:T(8,128)(2,1)} %fusion), kind=kOutput, calls=%fused_computation.89 | convolution fusion | flops 4295491584 | bytes 19922944 | tf_op jit(solution)/shard_map/scxp,ptq->tscxq/dot_general | solution.py:74
  144.3 23.1 %all_to_all.132 = bf16[16,2,16384]{2,1,0:T(2,128)(2,1)} all-to-all(bf16[16,2,16384]{2,1,0:T(2,128)(2,1)S(1)} %reshape.400), channel_id=1, replica_groups=mesh['dp'=8,'slab'=16] {'slab'}, dimensions={0} | all-to-all | bytes 2097152 | tf_op jit(solution)/shard_map/all_to_all | solution.py:78
  167.4 4.5 reshape.401
  174.7 3.7 copy.209
  181.1 6.6 %all-to-all-start.1 = ((bf16[8,2,32768]{2,1,0:T(2,128)(2,1)}), bf16[8,2,32768]{2,1,0:T(2,128)(2,1)}, u32[]{:S(2)}, u32[]{:S(2)}) async-start(bf16[8,2,32768]{2,1,0:T(2,128)(2,1)} %reshape.402), calls=%async_computation.1 | async-start | bytes 2097152 | tf_op jit(solution)/shard_map/all_to_all | solution.py:77
  187.7 4.0 fusion.142
  191.7 7.4 %copy.304 = bf16[1,64,64,256]{2,1,3,0:T(8,128)(2,1)} copy(bf16[1,64,64,256]{3,2,1,0:T(8,128)(2,1)} %get-tuple-element.37) | data formatting | bytes 4194304
  199.1 6.6 %copy.303 = bf16[1,64,64,256]{2,1,3,0:T(8,128)(2,1)} copy(bf16[1,64,64,256]{3,2,1,0:T(8,128)(2,1)S(1)} %get-tuple-element.36) | data formatting | bytes 4194304
  230.2 3.9 copy.224
  240.6 21.0 %all_to_all.133 = bf16[8,2,32768]{2,1,0:T(2,128)(2,1)} all-to-all(bf16[8,2,32768]{2,1,0:T(2,128)(2,1)S(1)} %reshape.404), channel_id=1, replica_groups=mesh['dp'=8,'slab'=16] {'dp'}, dimensions={0} | all-to-all | bytes 2097152 | tf_op jit(solution)/shard_map/all_to_all | solution.py:89
  261.6 4.3 reshape.405
  265.9 4.3 copy.336
  270.2 4.4 copy.227
  274.6 3.9 reshape.406
  278.5 22.5 %all_to_all.134 = bf16[16,2,16384]{2,1,0:T(2,128)(2,1)} all-to-all(bf16[16,2,16384]{2,1,0:T(2,128)(2,1)S(1)} %reshape.406), channel_id=1, replica_groups=mesh['dp'=8,'slab'=16] {'slab'}, dimensions={0} | all-to-all | bytes 2097152 | tf_op jit(solution)/shard_map/all_to_all | solution.py:88
  301.0 4.7 reshape.407
  313.4 10.5 %fusion.17 = f32[64,4,4096]{2,0,1:T(8,128)} fusion(bf16[2,64,4,1024]{3,1,0,2:T(8,128)(2,1)S(1)} %reshape.375, bf16[4096,2,1024]{2,0,1:T(8,128)(2,1)} %fusion), kind=kOutput, calls=%fused_computation.28 | convolution fusion | flops 4294967296 | bytes 22020096 | tf_op jit(solution)/shard_map/tscxq,ptq->scxp/dot_general | solution.py:95
  324.0 12.1 %convert_reduce_fusion = (f32[64]{0:T(128)S(1)}, bf16[1,64,4,4096]{3,1,2,0:T(8,128)(2,1)S(1)}, f32[64,4,4096]{2,0,1:T(8,128)}) fusion(bf16[1,64,4,4096]{3,2,1,0:T(4,128)(2,1)} %param.6, f32[64]{0:T(128)S(1)} %copy-done.13, f32[64,4,4096]{2,0,1:T(8,128)} %fusion.17, bf16[64,4,4096]{2,1,0:T(4,128)(2,1)} %bitcast.369, bf16[64,64]{1,0:T(8,128)(2,1)S(1)} %copy-done), kind=kOutput, calls=%fused_computation.64 | convolution fusion | flops 160432064 | bytes 14688768 | tf_op jit(solution)/shard_map/bixp,io->boxp/dot_general | solution.py:113
  337.4 8.3 %fusion.85 = bf16[2,1,64,4,1024]{4,2,3,0,1:T(8,128)(2,1)S(1)} fusion(bf16[1,64,4,4096]{3,1,2,0:T(8,128)(2,1)S(1)} %get-tuple-element.33, bf16[4096,2,1024]{2,0,1:T(8,128)(2,1)} %fusion), kind=kOutput, calls=%fused_computation.88 | convolution fusion | flops 4295491584 | bytes 19922944 | tf_op jit(solution)/shard_map/scxp,ptq->tscxq/dot_general | solution.py:74
  348.3 4.4 reshape.408
  352.7 20.0 %all_to_all.135 = bf16[16,2,16384]{2,1,0:T(2,128)(2,1)} all-to-all(bf16[16,2,16384]{2,1,0:T(2,128)(2,1)S(1)} %reshape.408), channel_id=1, replica_groups=mesh['dp'=8,'slab'=16] {'slab'}, dimensions={0} | all-to-all | bytes 2097152 | tf_op jit(solution)/shard_map/all_to_all | solution.py:78
  372.7 5.2 reshape.409
  377.9 4.1 copy.294
  382.0 4.4 copy.236
  386.4 4.3 reshape.410
  394.4 3.6 fusion.57
  403.5 66.4 %all-reduce = (f32[64,64]{0,1:T(8,128)S(1)}, f32[64]{0:T(128)S(1)}) all-reduce(f32[64,64]{0,1:T(8,128)S(1)} %fusion.111, f32[64]{0:T(128)S(1)} %get-tuple-element.32), channel_id=1, replica_groups=mesh['dp'=8,'slab'=16] {'dp','slab'}, use_global_device_ids=true, to_apply=%region_0.1 | all-reduce | flops 4160 | bytes 33280 | tf_op jit(solution)/shard_map/psum | solution.py:139
  473.8 4.2 copy.237
  482.2 5.4 fusion.35
  487.9 5.6 fusion.37
  496.2 4.8 fusion.100
  502.0 3.6 fusion.59
  505.5 3.9 copy.249
  512.6 4.3 reshape.412
  517.0 4.5 all-to-all-start.6
  526.1 9.3 %all-to-all-done.6 = bf16[8,2,32768]{2,1,0:T(2,128)(2,1)S(1)} async-done(((bf16[8,2,32768]{2,1,0:T(2,128)(2,1)}), bf16[8,2,32768]{2,1,0:T(2,128)(2,1)S(1)}, u32[]{:S(2)}, u32[]{:S(2)}) %all-to-all-start.6) | async-done | bytes 1048608 | tf_op jit(solution)/shard_map/all_to_all | solution.py:89
  538.1 4.3 copy.335
  542.4 4.4 copy.252
  546.8 4.6 reshape.414
  551.4 6.2 %all-to-all-start.7 = ((bf16[16,2,16384]{2,1,0:T(2,128)(2,1)}), bf16[16,2,16384]{2,1,0:T(2,128)(2,1)S(1)}, u32[]{:S(2)}, u32[]{:S(2)}) async-start(bf16[16,2,16384]{2,1,0:T(2,128)(2,1)} %reshape.414), calls=%async_computation.7 | async-start | bytes 2097152 | tf_op jit(solution)/shard_map/all_to_all | solution.py:88
  562.3 7.3 %pad_maximum_fusion = bf16[2,64,64,256]{1,2,3,0:T(8,128)(2,1)} fusion(bf16[1,64,64,256]{1,2,3,0:T(8,128)(2,1)S(1)} %copy-done.4, bf16[1,64,64,256]{1,2,3,0:T(8,128)(2,1)} %fusion.33), kind=kLoop, calls=%fused_computation.18 | loop fusion | flops 2097152 | bytes 8388608 | tf_op jit(solution)/shard_map/stack | solution.py:134
  569.6 13.5 %copy.266 = bf16[2,64,64,256]{3,2,1,0:T(8,128)(2,1)} copy(bf16[2,64,64,256]{1,2,3,0:T(8,128)(2,1)} %pad_maximum_fusion) | data formatting | bytes 8388608
  587.5 10.2 %fusion.14 = f32[64,4,4096]{2,0,1:T(8,128)} fusion(bf16[2,64,4,1024]{3,1,0,2:T(8,128)(2,1)S(1)} %reshape.379, bf16[4096,2,1024]{2,0,1:T(8,128)(2,1)} %fusion), kind=kOutput, calls=%fused_computation.27 | convolution fusion | flops 4294967296 | bytes 22020096 | tf_op jit(solution)/shard_map/tscxq,ptq->scxp/dot_general | solution.py:95
  (90 shorter events, 97.3 us)
Async XLA Ops:
  0.6 323.3 %copy-start = (bf16[64,64]{1,0:T(8,128)(2,1)S(1)}, bf16[64,64]{1,0:T(8,128)(2,1)}, u32[]{:S(2)}) copy-start(bf16[64,64]{1,0:T(8,128)(2,1)} %param.8) | copy-start | bytes 24580
  124.3 8.4 %copy-start.11 = (bf16[1,64,4,4096]{3,2,1,0:T(4,128)(2,1)S(1)}, bf16[1,64,4,4096]{3,2,1,0:T(4,128)(2,1)}, u32[]{:S(2)}) copy-start(bf16[1,64,4,4096]{3,2,1,0:T(4,128)(2,1)} %param.5) | copy-start | bytes 6291460
  181.1 25.0 %all-to-all-start.1 = ((bf16[8,2,32768]{2,1,0:T(2,128)(2,1)}), bf16[8,2,32768]{2,1,0:T(2,128)(2,1)}, u32[]{:S(2)}, u32[]{:S(2)}) async-start(bf16[8,2,32768]{2,1,0:T(2,128)(2,1)} %reshape.402), calls=%async_computation.1 | async-start | bytes 2097152 | tf_op jit(solution)/shard_map/all_to_all | solution.py:77
  206.1 9.0 %copy-start.9 = (bf16[4,4,2,64,2,32]{3,5,1,4,0,2:T(8,128)(2,1)}, bf16[4,4,2,64,2,32]{3,5,1,4,0,2:T(8,128)(2,1)S(1)}, u32[]{:S(2)}) copy-start(bf16[4,4,2,64,2,32]{3,5,1,4,0,2:T(8,128)(2,1)S(1)} %get-tuple-element.43) | copy-start | bytes 786436
  216.5 3.5 copy-start.3
  220.1 2.2 copy-start.1
  313.4 10.6 %copy-start.13 = (f32[64]{0:T(128)S(1)}, f32[64]{0:T(128)}, u32[]{:S(2)}) copy-start(f32[64]{0:T(128)} %param.9) | copy-start | bytes 772
  336.1 1.3 copy-start.6
  390.8 80.4 %all-to-all-start.5 = ((bf16[8,2,32768]{2,1,0:T(2,128)(2,1)}), bf16[8,2,32768]{2,1,0:T(2,128)(2,1)S(1)}, u32[]{:S(2)}, u32[]{:S(2)}) async-start(bf16[8,2,32768]{2,1,0:T(2,128)(2,1)} %reshape.410), calls=%async_computation.5 | async-start | bytes 2097152 | tf_op jit(solution)/shard_map/all_to_all | solution.py:77
  394.3 6.6 %copy-start.7 = (bf16[1,64,4,4096]{3,1,2,0:T(8,128)(2,1)S(1)}, bf16[1,64,4,4096]{3,1,2,0:T(8,128)(2,1)}, u32[]{:S(2)}) copy-start(bf16[1,64,4,4096]{3,1,2,0:T(8,128)(2,1)} %copy-done.6) | copy-start | bytes 6291460
  394.4 6.6 %copy-start.12 = (bf16[1,64,4,4096]{3,2,1,0:T(4,128)(2,1)S(1)}, bf16[1,64,4,4096]{3,2,1,0:T(4,128)(2,1)}, u32[]{:S(2)}) copy-start(bf16[1,64,4,4096]{3,2,1,0:T(4,128)(2,1)} %param.5) | copy-start | bytes 6291460
  473.8 7.2 %copy-start.10 = (bf16[4,4,2,64,2,32]{3,5,1,4,0,2:T(8,128)(2,1)S(1)}, bf16[4,4,2,64,2,32]{3,5,1,4,0,2:T(8,128)(2,1)}, u32[]{:S(2)}) copy-start(bf16[4,4,2,64,2,32]{3,5,1,4,0,2:T(8,128)(2,1)} %copy-done.9) | copy-start | bytes 786436
  487.9 5.6 copy-start.2
  487.9 5.6 copy-start.5
  517.0 18.5 %all-to-all-start.6 = ((bf16[8,2,32768]{2,1,0:T(2,128)(2,1)}), bf16[8,2,32768]{2,1,0:T(2,128)(2,1)S(1)}, u32[]{:S(2)}, u32[]{:S(2)}) async-start(bf16[8,2,32768]{2,1,0:T(2,128)(2,1)} %reshape.412), calls=%async_computation.6 | async-start | bytes 2097152 | tf_op jit(solution)/shard_map/all_to_all | solution.py:89
  551.4 31.7 %all-to-all-start.7 = ((bf16[16,2,16384]{2,1,0:T(2,128)(2,1)}), bf16[16,2,16384]{2,1,0:T(2,128)(2,1)S(1)}, u32[]{:S(2)}, u32[]{:S(2)}) async-start(bf16[16,2,16384]{2,1,0:T(2,128)(2,1)} %reshape.414), calls=%async_computation.7 | async-start | bytes 2097152 | tf_op jit(solution)/shard_map/all_to_all | solution.py:88
  558.9 3.3 copy-start.4
  587.5 10.2 %copy-start.8 = (bf16[1,64,4,4096]{3,1,2,0:T(8,128)(2,1)S(1)}, bf16[1,64,4,4096]{3,1,2,0:T(8,128)(2,1)}, u32[]{:S(2)}) copy-start(bf16[1,64,4,4096]{3,1,2,0:T(8,128)(2,1)} %copy-done.6) | copy-start | bytes 6291460
where the time goes:
time: 615 us; the launch traced here: 604 us
  local copies, waits for them, and re-layouts  221 us (36%)
  blocking collectives  153 us (25%)
  matrix products  99.6 us (16%)
  other arithmetic  98.5 us (16%)
  starting transfers between devices  20.8 us (3%)
  waiting for transfers between devices  9.35 us (2%)
    unnamed x50, local copies, waits for them, and re-layouts  94.1 us
    cos x1, other arithmetic, tables(): jnp.cos(angles)  66.8 us
    psum x1, blocking collectives, shards(): skip_total, bias_total = lax.psum((skip_part, bias_part), ('dp', 'slab'))  66.4 us
    add x2, local copies, waits for them, and re-layouts, tables(): phases[:, None, :, None] + phases[None, :, None, :]  45.4 us
    all_to_all x2, blocking collectives, to_spectrum(): lax.all_to_all(planes, 'slab', split_axis=4, concat_axis=3, tiled=True)  43 us
    all_to_all x1, blocking collectives, to_spatial(): lax.all_to_all(lax.all_to_all(lines, 'dp', split_axis=1, concat_axis=4, t...  22.5 us
    all_to_all x1, blocking collectives, to_spatial(): lax.all_to_all(lines, 'dp', split_axis=1, concat_axis=4, tiled=True)  21 us
    dot_general x2, matrix products, to_spatial(): jnp.einsum('tscxq,ptq->scxp', planes, plane_table, preferred_element_type...  20.8 us
  transfers between devices with their start and end apart: 4, of which 1 were waited for; matrix products, arithmetic and copies ran while one was open for 10% of the time, Pallas kernels for 0%

commit v1 on v0

v1 whole, which is shorter than its diff:
```python
import functools
import math

import jax
import jax.numpy as jnp
import ml_dtypes
import numpy as np
from jax import lax
from jax.experimental import pallas as pl
from jax.experimental.pallas import tpu as pltpu
from jax.sharding import PartitionSpec as P

N = 64
M = 32
C = 64
DP = 8
SLAB = 16
DEVICES = DP * SLAB
SAMPLES = 8
BF = jnp.bfloat16
F32 = jnp.float32
MESH = pl.DeviceIdType.MESH
VMEM_LIMIT = 56 * 1024 * 1024


def waves():
    phase = np.mod(np.arange(N)[:, None] * (np.arange(M)[None, :] - M // 2), N)
    angle = phase * (2.0 * math.pi / N)
    return np.cos(angle) / 8.0, np.sin(angle) / 8.0


def tables():
    cos, sin = waves()
    pair = np.stack([cos, -sin], 0).reshape(2, N, 4, 8)
    d1 = np.einsum("tzbl,uv->butlvz", pair, np.eye(4)).reshape(256, 256)
    turn = np.stack([np.stack([cos, sin], 0), np.stack([-sin, cos], 0)], 0)
    turn = turn.reshape(2, 2, N, SLAB, 2)
    d2 = np.einsum("stywx,el->xwseytl", turn, np.eye(8)).reshape(512, 1024)
    both = np.stack([cos, sin], 0)
    fwd = np.einsum("axk,ef->aekxf", both, np.eye(8)).reshape(512, 512)
    inv = np.einsum("axk,ef->axefk", both, np.eye(8)).reshape(1024, 256)
    out = (d1, d1.T, d2, d2.T, fwd, inv, np.eye(256))
    return tuple(np.ascontiguousarray(a).astype(ml_dtypes.bfloat16) for a in out)


def dot(a, b):
    return lax.dot_general(a, b, (((1,), (0,)), ((), ())), preferred_element_type=F32)


def dot_nt(a, b):
    return lax.dot_general(a, b, (((1,), (1,)), ((), ())), preferred_element_type=F32)


def low_lanes(shape):
    return lax.broadcasted_iota(jnp.int32, shape, len(shape) - 1) < 64


def swap(v):
    return pltpu.roll(v, 64, v.ndim - 1)


def signed_swap(v, low_sign):
    turned = swap(v)
    low = low_lanes(v.shape)
    return jnp.where(low, turned, -turned) if low_sign > 0 else jnp.where(low, -turned, turned)


def stage_y(b_ref, d2_ref, s_ref):
    def one(lb, carry):
        f = dot(d2_ref[...], b_ref[lb]).reshape(32, 2, 8, 256)
        t0 = f[:, 0]
        t1 = f[:, 1]
        parts = []
        for h in range(2):
            u0 = t0[:, :, 128 * h : 128 * h + 128]
            u1 = t1[:, :, 128 * h : 128 * h + 128]
            low = low_lanes(u0.shape)
            parts.append(jnp.where(low, u0, swap(u1)))
            parts.append(jnp.where(low, swap(u0), u1))
        chunk = jnp.stack(parts, 1).reshape(32, 32, 128).astype(BF)
        s_ref[pl.ds(lb * 16, 16)] = chunk[:16]
        s_ref[pl.ds(lb * 16 + 64, 16)] = chunk[16:]
        return carry

    lax.fori_loop(0, 4, one, 0)


def unstage_y(r_ref, d2t_ref, h_ref):
    def one(lb, carry):
        r = jnp.concatenate([r_ref[pl.ds(lb * 16, 16)], r_ref[pl.ds(lb * 16 + 64, 16)]], 0)
        r = r.astype(F32).reshape(32, 4, 8, 128)
        low = low_lanes((32, 8, 128))
        t0, t1 = [], []
        for h in range(2):
            r0 = r[:, 2 * h]
            r1 = r[:, 2 * h + 1]
            t0.append(jnp.where(low, r0, swap(r1)))
            t1.append(jnp.where(low, swap(r0), r1))
        t0 = jnp.concatenate(t0, 2)
        t1 = jnp.concatenate(t1, 2)
        rows = jnp.stack([t0, t1], 1).reshape(512, 256).astype(BF)
        h_ref[lb] = dot(d2t_ref[...], rows).astype(BF)
        return carry

    lax.fori_loop(0, 4, one, 0)


def store_quad(b_ref, quad, value):
    b_ref[:, pl.ds(pl.multiple_of(quad * 64, 64), 64), :] = value.astype(BF).reshape(4, 64, 256)


def load_quad(h_ref, quad):
    return h_ref[:, pl.ds(pl.multiple_of(quad * 64, 64), 64), :].reshape(256, 256)


def columns(quad):
    return pl.ds(pl.multiple_of(quad * 256, 256), 256)


def kernel_a(v_ref, d1_ref, d2_ref, s_ref, b_ref):
    def one(quad, carry):
        store_quad(b_ref, quad, dot_nt(d1_ref[...], v_ref[:, columns(quad)]))
        return carry

    lax.fori_loop(0, 16, one, 0)
    stage_y(b_ref, d2_ref, s_ref)


def line_forward(r_ref, fwd_ref, x_ref):
    for pair in range(4):
        a = r_ref[pl.ds(32 * pair, 16)].reshape(512, 128)
        b = r_ref[pl.ds(32 * pair + 16, 16)].reshape(512, 128)
        y = dot(fwd_ref[...], jnp.concatenate([a, b], 1))
        for h in range(2):
            lanes = slice(128 * h, 128 * h + 128)
            modes = y[:256, lanes] + signed_swap(y[256:, lanes], 1)
            x_ref[pl.ds(2 * pair + h, 256, stride=8), :] = modes.astype(BF).astype(F32)


def line_inverse(p_ref, inv_ref, s_ref):
    for pair in range(4):
        a = p_ref[pl.ds(2 * pair, 256, stride=8), :].astype(BF)
        b = p_ref[pl.ds(2 * pair + 1, 256, stride=8), :].astype(BF)
        y = dot(inv_ref[...], jnp.concatenate([a, b], 1))
        for h in range(2):
            lanes = slice(128 * h, 128 * h + 128)
            lines = y[:512, lanes] + signed_swap(y[512:, lanes], -1)
            s_ref[pl.ds(32 * pair + 16 * h, 16)] = lines.astype(BF).reshape(16, 32, 128)


def mix(x_ref, w_ref, p_ref):
    row_mode = lax.broadcasted_iota(jnp.int32, (32, 128), 0) // 8
    low = low_lanes((32, 128))

    def one(group, carry):
        x = x_ref[pl.ds(pl.multiple_of(group * 32, 32), 32), :]
        xs = swap(x)
        zero = jnp.zeros_like(x)
        top, bottom = [], []
        for h in range(2):
            even = jnp.logical_and(row_mode == 2 * h, low)
            odd = jnp.logical_and(row_mode == 2 * h + 1, jnp.logical_not(low))
            top.append(jnp.where(even, x, jnp.where(odd, xs, zero)))
            bottom.append(jnp.where(even, xs, jnp.where(odd, x, zero)))
        left = jnp.concatenate(
            [jnp.concatenate(top, 1), jnp.concatenate(bottom, 1)], 0
        ).astype(BF)
        w = w_ref[pl.ds(group * 4, 4)].reshape(256, 128)
        z = dot(left, w)
        p_ref[pl.ds(pl.multiple_of(group * 32, 32), 32), :] = z[:32] + signed_swap(z[32:], -1)
        return carry

    lax.fori_loop(0, 64, one, 0, unroll=4)


def mix_back(g_ref, w_ref, p_ref):
    row_mode = lax.broadcasted_iota(jnp.int32, (32, 128), 0) // 8
    low = low_lanes((32, 128))

    def one(group, carry):
        g = g_ref[pl.ds(pl.multiple_of(group * 32, 32), 32), :]
        left = jnp.concatenate([g, signed_swap(g, 1)], 0).astype(BF)
        w = w_ref[pl.ds(group * 4, 4)].reshape(256, 128)
        z = dot_nt(left, w)
        z0, z1 = z[:32], z[32:]
        even = row_mode % 2 == 0
        first = row_mode < 2
        a0 = jnp.where(first, z0[:, :128], z0[:, 128:])
        a1 = jnp.where(first, z1[:, :128], z1[:, 128:])
        b0 = jnp.where(even, a0, swap(a0))
        b1 = jnp.where(even, swap(a1), a1)
        p_ref[pl.ds(pl.multiple_of(group * 32, 32), 32), :] = jnp.where(low, b0, b1)
        return carry

    lax.fori_loop(0, 64, one, 0, unroll=4)


def kernel_c(r_ref, w_ref, fwd_ref, inv_ref, s_ref, x_ref, p_ref):
    line_forward(r_ref, fwd_ref, x_ref)
    mix(x_ref, w_ref, p_ref)
    line_inverse(p_ref, inv_ref, s_ref)


def kernel_g(r_ref, w_ref, fwd_ref, inv_ref, s_ref, x_ref, p_ref):
    line_forward(r_ref, fwd_ref, x_ref)
    mix_back(x_ref, w_ref, p_ref)
    line_inverse(p_ref, inv_ref, s_ref)


ROOT = math.sqrt(2.0 / math.pi)


def kernel_e(
    r_ref, v_ref, cot_ref, kron_ref, bias_ref, d1_ref, d1t_ref, d2_ref, d2t_ref, eye_ref,
    s_ref, out_ref, g_ref, part_ref, h_ref, b_ref, acc_ref, sum_ref,
):
    unstage_y(r_ref, d2t_ref, h_ref)
    acc_ref[...] = jnp.zeros_like(acc_ref)
    sum_ref[...] = jnp.zeros_like(sum_ref)

    def one(quad, carry):
        eye = eye_ref[...]
        v = v_ref[:, columns(quad)]
        vt = dot_nt(eye, v).astype(BF)
        pre = dot(d1t_ref[...], load_quad(h_ref, quad)) + dot(vt, kron_ref[...]) + bias_ref[...]
        square = pre * pre
        th = jnp.tanh(ROOT * pre * (1.0 + 0.044715 * square))
        half = 0.5 + 0.5 * th
        out = (pre * half).astype(BF)
        slope = half + 0.5 * pre * (1.0 - th * th) * (ROOT + (3.0 * 0.044715 * ROOT) * square)
        cot = dot_nt(eye, cot_ref[:, columns(quad)])
        g = (cot * slope).astype(BF)
        g_ref[columns(quad), :] = g
        store_quad(b_ref, quad, dot(d1_ref[...], g))
        out_ref[:, columns(quad)] = dot_nt(eye, out).astype(BF)
        acc_ref[...] += dot(v, g)
        sum_ref[...] += jnp.sum(g.astype(F32).reshape(32, 8, 256), axis=0)
        return carry

    lax.fori_loop(0, 16, one, 0)
    stage_y(b_ref, d2_ref, s_ref)
    acc = acc_ref[...]
    low = low_lanes((64, 128))
    a = acc[:64, :128] + acc[128:192, 128:]
    b = acc[64:128, :128] + acc[192:, 128:]
    part_ref[pl.ds(0, 64), :] = jnp.where(low, a + swap(b), 0.0)
    line = jnp.sum(sum_ref[...], axis=0, keepdims=True)
    line = line[:, :128] + line[:, 128:]
    line = line + swap(line)
    part_ref[pl.ds(64, 8), :] = jnp.broadcast_to(line, (8, 128))


def kernel_i(r_ref, g_ref, kron_ref, d1t_ref, d2t_ref, eye_ref, out_ref, h_ref):
    unstage_y(r_ref, d2t_ref, h_ref)

    def one(quad, carry):
        value = dot(d1t_ref[...], load_quad(h_ref, quad)) + dot(g_ref[columns(quad), :], kron_ref[...])
        out_ref[:, columns(quad)] = dot_nt(eye_ref[...], value.astype(BF)).astype(BF)
        return carry

    lax.fori_loop(0, 16, one, 0)


def kernel_w(x_ref, g_ref, eye_ref, out_ref, a_ref):
    lane_mode = (lax.broadcasted_iota(jnp.int32, (64, 256), 1) // 8) % 16

    def one(group, carry):
        rows = pl.ds(pl.multiple_of(group * 128, 128), 128)
        xt = x_ref[rows, :].T
        xt = jnp.concatenate([xt[:64], xt[64:]], 1)
        g = g_ref[rows, :]
        right = jnp.concatenate([g, signed_swap(g, 1)], 0).astype(BF)
        left = jnp.concatenate(
            [jnp.where(lane_mode == m, xt, 0.0) for m in range(16)], 0
        ).astype(BF)
        a_ref[pl.ds(pl.multiple_of(group * 1024, 1024), 1024), :] = dot(left, right)
        return carry

    lax.fori_loop(0, 16, one, 0)

    def turn(i, carry):
        value = a_ref[pl.ds(i, 256, stride=64), :].astype(BF)
        plane = dot_nt(eye_ref[pl.ds(0, 128), pl.ds(0, 128)], value).astype(BF)
        out_ref[0, i] = plane[:64]
        out_ref[1, i] = plane[64:]
        return carry

    lax.fori_loop(0, 64, turn, 0, unroll=2)


def kernel_exchange(x_ref, o_ref, send_sem, recv_sem, local_sem):
    dp = lax.axis_index("dp")
    slab = lax.axis_index("slab")
    me = dp * SLAB + slab

    def partner(i):
        step = (i * 37) % DEVICES
        return (dp + step // SLAB) % DP, (slab + step % SLAB) % SLAB

    barrier = pltpu.get_barrier_semaphore()

    def greet(i, carry):
        pl.semaphore_signal(barrier, inc=1, device_id=partner(i), device_id_type=MESH)
        return carry

    lax.fori_loop(1, DEVICES, greet, 0)
    local = pltpu.make_async_copy(x_ref.at[me], o_ref.at[me], local_sem)
    local.start()
    pl.semaphore_wait(barrier, DEVICES - 1)

    def send(i, carry):
        to = partner(i)
        pltpu.make_async_remote_copy(
            src_ref=x_ref.at[to[0] * SLAB + to[1]],
            dst_ref=o_ref.at[me],
            send_sem=send_sem,
            recv_sem=recv_sem,
            device_id=to,
            device_id_type=MESH,
        ).start()
        return carry

    lax.fori_loop(1, DEVICES, send, 0)
    local.wait()
    rest = pl.ds(0, DEVICES - 1)
    pltpu.make_async_copy(x_ref.at[rest], x_ref.at[rest], send_sem).wait()
    pltpu.make_async_copy(o_ref.at[rest], o_ref.at[rest], recv_sem).wait()


WHOLE = pl.BlockSpec(memory_space=pltpu.VMEM)
CHUNKS = jax.ShapeDtypeStruct((DEVICES, 32, 128), BF)


def exchange(x, number):
    return pl.pallas_call(
        kernel_exchange,
        out_shape=CHUNKS,
        in_specs=[WHOLE],
        out_specs=WHOLE,
        scratch_shapes=[pltpu.SemaphoreType.DMA] * 3,
        compiler_params=pltpu.CompilerParams(collective_id=number, has_side_effects=True),
        name="exchange_%d" % number,
    )(x)


def call(kernel, out_shape, scratch, *args):
    several = isinstance(out_shape, (tuple, list))
    return pl.pallas_call(
        kernel,
        out_shape=out_shape,
        in_specs=[WHOLE] * len(args),
        out_specs=[WHOLE] * len(out_shape) if several else WHOLE,
        scratch_shapes=scratch,
        compiler_params=pltpu.CompilerParams(vmem_limit_bytes=VMEM_LIMIT),
        name=kernel.__name__,
    )(*args)


def shards(field, cotangent, spectral, skip, bias):
    d1, d1t, d2, d2t, fwd, inv, eye = (jnp.asarray(a) for a in tables())
    shape = lambda dims, dtype: jax.ShapeDtypeStruct(dims, dtype)
    half = pltpu.VMEM((4, 1024, 256), BF)
    modes = shape((2048, 128), F32)

    v = jnp.transpose(field[0], (1, 0, 2)).reshape(256, N * N)
    cot = jnp.transpose(cotangent[0], (1, 0, 2)).reshape(256, N * N)
    w = jnp.transpose(spectral, (3, 1, 0, 2)).reshape(256, C, 2 * C)
    unit = jnp.eye(4, dtype=BF)
    kron = jnp.einsum("xy,io->xiyo", unit, skip).reshape(256, 256)
    kron_back = jnp.einsum("xy,io->xoyi", unit, skip).reshape(256, 256)
    bias_row = jnp.tile(bias, 4).reshape(1, 256)

    s1 = call(kernel_a, CHUNKS, [half], v, d1, d2)
    r1 = exchange(s1, 1)
    s2, x = call(kernel_c, (CHUNKS, modes), [pltpu.VMEM((2048, 128), F32)], r1, w, fwd, inv)
    r2 = exchange(s2, 2)
    s3, out, g, part = call(
        kernel_e,
        (CHUNKS, shape((256, N * N), BF), shape((N * N, 256), BF), shape((72, 128), F32)),
        [half, half, pltpu.VMEM((256, 256), F32), pltpu.VMEM((8, 256), F32)],
        r2, v, cot, kron, bias_row, d1, d1t, d2, d2t, eye,
    )
    r3 = exchange(s3, 3)
    s4, gm = call(kernel_g, (CHUNKS, modes), [pltpu.VMEM((2048, 128), F32)], r3, w, fwd, inv)
    r4 = exchange(s4, 4)
    spectral_grad = call(
        kernel_w, shape((2, C, C, 256), BF), [pltpu.VMEM((256 * 64, 128), F32)], x, gm, eye
    )
    back = call(kernel_i, shape((256, N * N), BF), [half], r4, g, kron_back, d1t, d2t, eye)

    total = lax.psum(part[:65, :64], ("dp", "slab")) * (1.0 / math.sqrt(SAMPLES * N * N * N))
    spread = lambda a: jnp.transpose(a.reshape(4, C, N * N), (1, 0, 2))[None]
    return (spread(out), spread(back), spectral_grad, total[:64], total[64])


def solution(mesh):
    whole = P("dp", None, "slab", None)
    modes = P(None, None, None, ("slab", "dp"))
    return jax.shard_map(
        shards,
        mesh=mesh,
        in_specs=(whole, whole, modes, P(), P()),
        out_specs=(whole, whole, modes, P(), P()),
        check_vma=False,
    )
```

time: 615 us -> 284 us (0.46); the launches traced: 604 us -> 284 us
  local copies, waits for them, and re-layouts: 221 us -> 29.9 us
  Pallas kernels: 0 us -> 188 us
  matrix products: 99.6 us -> 0 us
  other arithmetic: 98.5 us -> 0.23 us
  blocking collectives: 153 us -> 64.3 us
  starting transfers between devices: 20.8 us -> 0 us
  waiting for transfers between devices: 9.35 us -> 0 us
    pallas_call x0 -> x10, Pallas kernels: none -> 188 us  [the longest x4 104 us: exchange(): pl.pallas_call(kernel_exchange, out_shape=CHUNKS, in_specs=[WHOLE], out_s...]
    dot_general x23 -> x0, matrix products: 99.6 us -> none  [the longest x2 20.8 us: to_spatial(): jnp.einsum('tscxq,ptq->scxp', planes, plane_table, preferred_element_type...]
    unnamed x50 -> x8, local copies, waits for them, and re-layouts: 94.1 us -> 3.14 us
    all_to_all x4 -> x0, blocking collectives: 86.5 us -> none  [the longest x2 43 us: to_spectrum(): lax.all_to_all(planes, 'slab', split_axis=4, concat_axis=3, tiled=True)]
    cos x1 -> x0, other arithmetic: 66.8 us -> none  [tables(): jnp.cos(angles)]
    all_to_all x16 -> x0, local copies, waits for them, and re-layouts: 51.4 us -> none  [the longest x4 17.3 us: to_spatial(): lax.all_to_all(lines, 'dp', split_axis=1, concat_axis=4, tiled=True)]
    add x2 -> x0, local copies, waits for them, and re-layouts: 45.4 us -> none  [tables(): phases[:, None, :, None] + phases[None, :, None, :]]
    all_to_all x4 -> x0, starting transfers between devices: 20.8 us -> none  [the longest x2 10.1 us: to_spectrum(): lax.all_to_all(lax.all_to_all(planes, 'slab', split_axis=4, concat_axis=3...]
  transfers between devices with their start and end apart: 4 -> 0, of which waited for: 1 -> 0; matrix products, arithmetic and copies ran while one was open for 10% -> 0% of each run, Pallas kernels for 0% -> 0%
where the time goes in v1:
time: 284 us
  Pallas kernels  188 us (66%)
  blocking collectives  64.3 us (23%)
  local copies, waits for them, and re-layouts  29.9 us (11%)
    pallas_call x4, Pallas kernels, exchange(): pl.pallas_call(kernel_exchange, out_shape=CHUNKS, in_specs=[WHOLE], out_s...  104 us
    pallas_call x6, Pallas kernels, call(): pl.pallas_call(kernel, out_shape=out_shape, in_specs=[WHOLE] * len(args),...  84.7 us
    psum x1, blocking collectives, shards(): lax.psum(part[:65, :64], ('dp', 'slab'))  64.3 us
    broadcast_in_dim x1, local copies, waits for them, and re-layouts, shards(): spread = lambda a: jnp.transpose(a.reshape(4, C, N * N), (1, 0, 2))[None]  9.29 us
    reshape x1, local copies, waits for them, and re-layouts, shards(): w = jnp.transpose(spectral, (3, 1, 0, 2)).reshape(256, C, 2 * C)  6.55 us

profile of v1, /device:TPU:1, one launch (start us, length us, event | category | flops | bytes accessed | tf_op | source)
XLA Modules:
  0.0 283.5 jit_solution(524543349346034373)
XLA Ops:
  0.6 0.7 tile.2
  1.3 0.6 reshape_tile.3.bias_ref
  1.9 0.8 copy.28
  2.7 0.2 multiply_bitcast_fusion
  3.0 0.9 reshape.37.kron_ref
  3.8 0.2 copy.29
  4.1 0.9 reshape.35.kron_ref
  4.9 4.1 %copy.24 = bf16[4,64,4096]{2,1,0:T(8,128)(2,1)} copy(bf16[4,64,4096]{2,0,1:T(4,128)(2,1)} %bitcast.33) | data formatting | bytes 4194304 | tf_op jit(solution)/shard_map/transpose | solution.py:365
  9.0 8.6 %kernel_a.1.x_ref = bf16[128,32,128]{2,1,0:T(8,128)(2,1)} custom-call(bf16[256,4096]{1,0:T(8,128)(2,1)} %bitcast.28, bf16[256,256]{1,0:T(8,128)(2,1)} %constant.16.clone.d1_ref, bf16[512,1024]{1,0:T(8,128)(2,1)} %constant.18.clone.d2_ref), custom_call_target="tpu_custom_call" | custom-call | tf_op jit(solution)/shard_map/kernel_a/pallas_call | solution.py:348
  17.6 0.0 copy-start.1
  17.6 29.1 %exchange_1.1.r_ref = bf16[128,32,128]{2,1,0:T(8,128)(2,1)} custom-call(bf16[128,32,128]{2,1,0:T(8,128)(2,1)} %kernel_a.1.x_ref), custom_call_target="tpu_custom_call" | custom-call | tf_op jit(solution)/shard_map/exchange_1/pallas_call | solution.py:335
  46.7 0.0 copy-done.1
  46.8 0.0 copy-start
  46.8 2.5 copy.27
  49.2 0.0 copy-done
  49.2 2.3 copy.25
  51.6 6.5 %copy.26.w_ref = bf16[256,64,128]{2,1,0:T(8,128)(2,1)} copy(bf16[256,64,128]{0,2,1:T(8,128)(2,1)} %bitcast.30) | data formatting | bytes 8388608 | tf_op jit(solution)/shard_map/reshape | solution.py:367
  58.1 10.5 %kernel_c.1 = (bf16[128,32,128]{2,1,0:T(8,128)(2,1)}, f32[2048,128]{1,0:T(8,128)}) custom-call(bf16[128,32,128]{2,1,0:T(8,128)(2,1)} %exchange_1.1.r_ref, bf16[256,64,128]{2,1,0:T(8,128)(2,1)} %copy.26.w_ref, bf16[512,512]{1,0:T(8,128)(2,1)} %constant.20.clone.fwd_ref, bf16[1024,256]{1,0:T(8,128)(2,1)} %constant.21.clone.inv_ref), custom_call_target="tpu_custom_call" | custom-call | tf_op jit(solution)/shard_map/kernel_c/pallas_call | solution.py:348
  68.6 25.1 %exchange_2.1.r_ref = bf16[128,32,128]{2,1,0:T(8,128)(2,1)} custom-call(bf16[128,32,128]{2,1,0:T(8,128)(2,1)} %get-tuple-element.13.x_ref), custom_call_target="tpu_custom_call" | custom-call | tf_op jit(solution)/shard_map/exchange_2/pallas_call | solution.py:335
  93.7 22.7 %kernel_e.1 = (bf16[128,32,128]{2,1,0:T(8,128)(2,1)}, bf16[256,4096]{1,0:T(8,128)(2,1)}, bf16[4096,256]{1,0:T(8,128)(2,1)}, f32[72,128]{1,0:T(8,128)}) custom-call(bf16[128,32,128]{2,1,0:T(8,128)(2,1)} %exchange_2.1.r_ref, bf16[256,4096]{1,0:T(8,128)(2,1)} %bitcast.29, bf16[256,4096]{1,0:T(8,128)(2,1)} %bitcast.32, bf16[256,256]{1,0:T(8,128)(2,1)} %reshape.35.kron_ref, ...), custom_call_target="tpu_custom_call" | custom-call | tf_op jit(solution)/shard_map/kernel_e/pallas_call | solution.py:348
  116.4 64.3 %psum.7 = f32[65,64]{1,0:T(8,128)S(1)} all-reduce(f32[65,64]{1,0:T(8,128)} %bitcast.36), channel_id=1, replica_groups=mesh['dp'=8,'slab'=16] {'dp','slab'}, use_global_device_ids=true, to_apply=%region_0.0 | all-reduce | flops 4160 | bytes 33280 | tf_op jit(solution)/shard_map/psum | solution.py:391
  180.7 0.5 slice_bitcast_fusion
  181.2 0.6 slice.12
  181.8 24.6 %exchange_3.1.r_ref = bf16[128,32,128]{2,1,0:T(8,128)(2,1)} custom-call(bf16[128,32,128]{2,1,0:T(8,128)(2,1)} %get-tuple-element.15.x_ref), custom_call_target="tpu_custom_call" | custom-call | tf_op jit(solution)/shard_map/exchange_3/pallas_call | solution.py:335
  206.4 10.3 %kernel_g.1 = (bf16[128,32,128]{2,1,0:T(8,128)(2,1)}, f32[2048,128]{1,0:T(8,128)}) custom-call(bf16[128,32,128]{2,1,0:T(8,128)(2,1)} %exchange_3.1.r_ref, bf16[256,64,128]{2,1,0:T(8,128)(2,1)} %copy.26.w_ref, bf16[512,512]{1,0:T(8,128)(2,1)} %constant.20.clone.fwd_ref, bf16[1024,256]{1,0:T(8,128)(2,1)} %constant.21.clone.inv_ref), custom_call_target="tpu_custom_call" | custom-call | tf_op jit(solution)/shard_map/kernel_g/pallas_call | solution.py:348
  216.7 25.0 %exchange_4.1.r_ref = bf16[128,32,128]{2,1,0:T(8,128)(2,1)} custom-call(bf16[128,32,128]{2,1,0:T(8,128)(2,1)} %get-tuple-element.16.x_ref), custom_call_target="tpu_custom_call" | custom-call | tf_op jit(solution)/shard_map/exchange_4/pallas_call | solution.py:335
  241.7 0.0 copy-start.2
  241.7 13.4 %kernel_i.1 = bf16[256,4096]{1,0:T(8,128)(2,1)} custom-call(bf16[128,32,128]{2,1,0:T(8,128)(2,1)} %exchange_4.1.r_ref, bf16[4096,256]{1,0:T(8,128)(2,1)} %get-tuple-element.17.g_ref, bf16[256,256]{1,0:T(8,128)(2,1)} %reshape.37.kron_ref, bf16[256,256]{1,0:T(8,128)(2,1)} %constant.17.clone.d1t_ref, bf16[1024,512]{1,0:T(8,128)(2,1)} %constant.19.clone.d2t_ref, ...), custom_call_target="tpu_custom_call" | custom-call | tf_op jit(solution)/shard_map/kernel_i/pallas_call | solution.py:348
  255.1 0.0 copy-done.2
  255.1 9.3 %copy_bitcast_fusion = (bf16[1,64,4,4096]{3,2,1,0:T(4,128)(2,1)}, bf16[1,64,4,4096]{3,2,1,0:T(4,128)(2,1)}) fusion(bf16[4,64,4096]{2,1,0:T(8,128)(2,1)} %bitcast.31, bf16[4,64,4096]{2,1,0:T(8,128)(2,1)S(1)} %bitcast.35), kind=kLoop, calls=%fused_computation | loop fusion | bytes 8388608 | tf_op jit(solution)/shard_map/broadcast_in_dim | solution.py:392
  264.4 19.1 %kernel_w.1 = bf16[2,64,64,256]{3,2,1,0:T(8,128)(2,1)} custom-call(f32[2048,128]{1,0:T(8,128)} %get-tuple-element.18.x_ref, f32[2048,128]{1,0:T(8,128)} %get-tuple-element.19.g_ref, bf16[256,256]{1,0:T(8,128)(2,1)} %constant.22.clone.eye_ref), custom_call_target="tpu_custom_call" | custom-call | tf_op jit(solution)/shard_map/kernel_w/pallas_call | solution.py:348
  (2 shorter events, 0.0 us)
Async XLA Ops:
  17.6 29.1 %copy-start.1 = (bf16[1,64,4,4096]{3,2,1,0:T(4,128)(2,1)S(1)}, bf16[1,64,4,4096]{3,2,1,0:T(4,128)(2,1)}, u32[]{:S(2)}) copy-start(bf16[1,64,4,4096]{3,2,1,0:T(4,128)(2,1)} %param.13) | copy-start | bytes 6291460
  46.8 2.5 copy-start
  241.7 13.4 %copy-start.2 = (bf16[256,4096]{1,0:T(8,128)(2,1)S(1)}, bf16[256,4096]{1,0:T(8,128)(2,1)}, u32[]{:S(2)}) copy-start(bf16[256,4096]{1,0:T(8,128)(2,1)} %get-tuple-element.14) | copy-start | bytes 6291460

commit v2 on v1

v2 whole, which is shorter than its diff:
```python
import functools
import math

import jax
import jax.numpy as jnp
import ml_dtypes
import numpy as np
from jax import lax
from jax.experimental import pallas as pl
from jax.experimental.pallas import tpu as pltpu
from jax.sharding import PartitionSpec as P

N = 64
M = 32
C = 64
DP = 8
SLAB = 16
DEVICES = DP * SLAB
SAMPLES = 8
BF = jnp.bfloat16
F32 = jnp.float32
MESH = pl.DeviceIdType.MESH
VMEM_LIMIT = 56 * 1024 * 1024


def waves():
    phase = np.mod(np.arange(N)[:, None] * (np.arange(M)[None, :] - M // 2), N)
    angle = phase * (2.0 * math.pi / N)
    return np.cos(angle) / 8.0, np.sin(angle) / 8.0


def tables():
    cos, sin = waves()
    pair = np.stack([cos, -sin], 0).reshape(2, N, 4, 8)
    d1 = np.einsum("tzbl,uv->butlvz", pair, np.eye(4)).reshape(256, 256)
    turn = np.stack([np.stack([cos, sin], 0), np.stack([-sin, cos], 0)], 0)
    turn = turn.reshape(2, 2, N, SLAB, 2)
    d2 = np.einsum("stywx,el->xwseytl", turn, np.eye(8)).reshape(512, 1024)
    both = np.stack([cos, sin], 0)
    fwd = np.einsum("axk,ef->aekxf", both, np.eye(8)).reshape(512, 512)
    inv = np.einsum("axk,ef->axefk", both, np.eye(8)).reshape(1024, 256)
    out = (d1, d1.T, d2, d2.T, fwd, inv, np.eye(256))
    return tuple(np.ascontiguousarray(a).astype(ml_dtypes.bfloat16) for a in out)


def dot(a, b):
    return lax.dot_general(a, b, (((1,), (0,)), ((), ())), preferred_element_type=F32)


def dot_nt(a, b):
    return lax.dot_general(a, b, (((1,), (1,)), ((), ())), preferred_element_type=F32)


def low_lanes(shape):
    return lax.broadcasted_iota(jnp.int32, shape, len(shape) - 1) < 64


def swap(v):
    return pltpu.roll(v, 64, v.ndim - 1)


def signed_swap(v, low_sign):
    turned = swap(v)
    low = low_lanes(v.shape)
    return jnp.where(low, turned, -turned) if low_sign > 0 else jnp.where(low, -turned, turned)


def stage_y(b_ref, d2_ref, s_ref, first, send):
    def one(k, carry):
        lb = (first + k) % 4
        f = dot(d2_ref[...], b_ref[lb]).reshape(32, 2, 8, 256)
        t0 = f[:, 0]
        t1 = f[:, 1]
        parts = []
        for h in range(2):
            u0 = t0[:, :, 128 * h : 128 * h + 128]
            u1 = t1[:, :, 128 * h : 128 * h + 128]
            low = low_lanes(u0.shape)
            parts.append(jnp.where(low, u0, swap(u1)))
            parts.append(jnp.where(low, swap(u0), u1))
        chunk = jnp.stack(parts, 1).reshape(32, 32, 128).astype(BF)
        s_ref[pl.ds(lb * 16, 16)] = chunk[:16]
        s_ref[pl.ds(lb * 16 + 64, 16)] = chunk[16:]
        send(lb)
        send(lb + 4)
        return carry

    lax.fori_loop(0, 4, one, 0)


def unstage_y(r_ref, d2t_ref, h_ref):
    def one(lb, carry):
        r = jnp.concatenate([r_ref[pl.ds(lb * 16, 16)], r_ref[pl.ds(lb * 16 + 64, 16)]], 0)
        r = r.astype(F32).reshape(32, 4, 8, 128)
        low = low_lanes((32, 8, 128))
        t0, t1 = [], []
        for h in range(2):
            r0 = r[:, 2 * h]
            r1 = r[:, 2 * h + 1]
            t0.append(jnp.where(low, r0, swap(r1)))
            t1.append(jnp.where(low, swap(r0), r1))
        t0 = jnp.concatenate(t0, 2)
        t1 = jnp.concatenate(t1, 2)
        rows = jnp.stack([t0, t1], 1).reshape(512, 256).astype(BF)
        h_ref[lb] = dot(d2t_ref[...], rows).astype(BF)
        return carry

    lax.fori_loop(0, 4, one, 0)


def store_quad(b_ref, quad, value):
    b_ref[:, pl.ds(pl.multiple_of(quad * 64, 64), 64), :] = value.astype(BF).reshape(4, 64, 256)


def load_quad(h_ref, quad):
    return h_ref[:, pl.ds(pl.multiple_of(quad * 64, 64), 64), :].reshape(256, 256)


def columns(quad):
    return pl.ds(pl.multiple_of(quad * 256, 256), 256)


def line_forward(r_ref, fwd_ref, x_ref):
    def one(pair, carry):
        a = r_ref[pl.ds(32 * pair, 16)].reshape(512, 128)
        b = r_ref[pl.ds(32 * pair + 16, 16)].reshape(512, 128)
        y = dot(fwd_ref[...], jnp.concatenate([a, b], 1))
        for h in range(2):
            lanes = slice(128 * h, 128 * h + 128)
            modes = y[:256, lanes] + signed_swap(y[256:, lanes], 1)
            x_ref[pl.ds(2 * pair + h, 256, stride=8), :] = modes.astype(BF).astype(F32)
        return carry

    lax.fori_loop(0, 4, one, 0)


def line_inverse(p_ref, inv_ref, s_ref, first, send):
    def one(k, carry):
        pair = (first + k) % 4
        a = p_ref[pl.ds(2 * pair, 256, stride=8), :].astype(BF)
        b = p_ref[pl.ds(2 * pair + 1, 256, stride=8), :].astype(BF)
        y = dot(inv_ref[...], jnp.concatenate([a, b], 1))
        for h in range(2):
            lanes = slice(128 * h, 128 * h + 128)
            lines = y[:512, lanes] + signed_swap(y[512:, lanes], -1)
            s_ref[pl.ds(32 * pair + 16 * h, 16)] = lines.astype(BF).reshape(16, 32, 128)
        send(2 * pair)
        send(2 * pair + 1)
        return carry

    lax.fori_loop(0, 4, one, 0)


def mix(x_ref, w_ref, p_ref):
    row_mode = lax.broadcasted_iota(jnp.int32, (32, 128), 0) // 8
    low = low_lanes((32, 128))

    def one(group, carry):
        x = x_ref[pl.ds(pl.multiple_of(group * 32, 32), 32), :]
        xs = swap(x)
        zero = jnp.zeros_like(x)
        top, bottom = [], []
        for h in range(2):
            even = jnp.logical_and(row_mode == 2 * h, low)
            odd = jnp.logical_and(row_mode == 2 * h + 1, jnp.logical_not(low))
            top.append(jnp.where(even, x, jnp.where(odd, xs, zero)))
            bottom.append(jnp.where(even, xs, jnp.where(odd, x, zero)))
        left = jnp.concatenate(
            [jnp.concatenate(top, 1), jnp.concatenate(bottom, 1)], 0
        ).astype(BF)
        w = w_ref[pl.ds(pl.multiple_of(group * 256, 256), 256), :].astype(BF)
        z = dot(left, w)
        p_ref[pl.ds(pl.multiple_of(group * 32, 32), 32), :] = z[:32] + signed_swap(z[32:], -1)
        return carry

    lax.fori_loop(0, 64, one, 0, unroll=4)


def mix_back(g_ref, w_ref, p_ref):
    row_mode = lax.broadcasted_iota(jnp.int32, (32, 128), 0) // 8
    low = low_lanes((32, 128))

    def one(group, carry):
        g = g_ref[pl.ds(pl.multiple_of(group * 32, 32), 32), :]
        left = jnp.concatenate([g, signed_swap(g, 1)], 0).astype(BF)
        w = w_ref[pl.ds(pl.multiple_of(group * 256, 256), 256), :].astype(BF)
        z = dot_nt(left, w)
        z0, z1 = z[:32], z[32:]
        even = row_mode % 2 == 0
        first = row_mode < 2
        a0 = jnp.where(first, z0[:, :128], z0[:, 128:])
        a1 = jnp.where(first, z1[:, :128], z1[:, 128:])
        b0 = jnp.where(even, a0, swap(a0))
        b1 = jnp.where(even, swap(a1), a1)
        p_ref[pl.ds(pl.multiple_of(group * 32, 32), 32), :] = jnp.where(low, b0, b1)
        return carry

    lax.fori_loop(0, 64, one, 0, unroll=4)


ROOT = math.sqrt(2.0 / math.pi)
FACTOR = 1.0 / math.sqrt(SAMPLES * N * N * N)


def turn_weights(raw_ref, eye_ref, w_ref):
    def one(i, carry):
        plane = jnp.concatenate([raw_ref[0, i], raw_ref[1, i]], 0)
        w_ref[pl.ds(i, 256, stride=64), :] = dot_nt(eye_ref[...], plane)
        return carry

    lax.fori_loop(0, 64, one, 0, unroll=2)


def weight_gradient(x_ref, g_ref, eye_ref, out_ref, a_ref):
    lane_mode = (lax.broadcasted_iota(jnp.int32, (64, 256), 1) // 8) % 16

    def one(group, carry):
        rows = pl.ds(pl.multiple_of(group * 128, 128), 128)
        xt = x_ref[rows, :].T
        xt = jnp.concatenate([xt[:64], xt[64:]], 1)
        g = g_ref[rows, :]
        right = jnp.concatenate([g, signed_swap(g, 1)], 0).astype(BF)
        left = jnp.concatenate(
            [jnp.where(lane_mode == m, xt, 0.0) for m in range(16)], 0
        ).astype(BF)
        a_ref[pl.ds(pl.multiple_of(group * 1024, 1024), 1024), :] = dot(left, right)
        return carry

    lax.fori_loop(0, 16, one, 0)

    def turn(i, carry):
        value = a_ref[pl.ds(i, 256, stride=64), :].astype(BF)
        plane = dot_nt(eye_ref[pl.ds(0, 128), pl.ds(0, 128)], value).astype(BF)
        out_ref[0, i] = plane[:64]
        out_ref[1, i] = plane[64:]
        return carry

    lax.fori_loop(0, 64, turn, 0, unroll=2)


def layer(
    v_ref, cot_hbm, raw_hbm, kron_ref, kron_back_ref, bias_ref,
    d1_ref, d1t_ref, d2_ref, d2t_ref, fwd_ref, inv_ref, eye_ref,
    out_hbm, back_ref, sg_hbm, skip_ref, line_ref,
    cot_ref, raw_ref, out_ref, sg_ref, g_ref, h_ref, b_ref, w_ref, x_ref, y_ref, p_ref,
    acc_ref, sum_ref, part_ref, slab_ref, half_ref, dp_ref, total_ref,
    s1, s2, r1, r2, r3, r4,
    send_sem, recv_sem, local_sem, load_sem, store_sem, small_send, small_recv,
):
    dp = lax.axis_index("dp")
    slab = lax.axis_index("slab")
    me = dp * SLAB + slab

    def wait_bytes(ref, sem):
        pltpu.make_async_copy(ref, ref, sem).wait()

    barrier = pltpu.get_barrier_semaphore()

    def greet(i, carry):
        to = ((dp + i // SLAB) % DP, (slab + i % SLAB) % SLAB)
        pl.semaphore_signal(barrier, inc=1, device_id=to, device_id_type=MESH)
        return carry

    lax.fori_loop(1, DEVICES, greet, 0)
    load_cot = pltpu.make_async_copy(cot_hbm, cot_ref, load_sem.at[0])
    load_raw = pltpu.make_async_copy(raw_hbm, raw_ref, load_sem.at[1])
    load_raw.start()
    load_cot.start()

    def sender(s_ref, r_ref, phase):
        def remote(row, step):
            column = (slab + step) % SLAB
            return pltpu.make_async_remote_copy(
                src_ref=s_ref.at[row * SLAB + column],
                dst_ref=r_ref.at[me],
                send_sem=send_sem.at[phase],
                recv_sem=recv_sem.at[phase],
                device_id=(row, column),
                device_id_type=MESH,
            )

        def send(row):
            def one(step, carry):
                remote(row, step).start()
                return carry

            lax.fori_loop(1, SLAB, one, 0)

            @pl.when(row != dp)
            def _():
                remote(row, 0).start()

            @pl.when(row == dp)
            def _():
                pltpu.make_async_copy(s_ref.at[me], r_ref.at[me], local_sem.at[phase]).start()

        return send

    rest = pl.ds(0, DEVICES - 1)

    def arrived(s_ref, r_ref, phase):
        pltpu.make_async_copy(s_ref.at[me], r_ref.at[me], local_sem.at[phase]).wait()
        wait_bytes(s_ref.at[rest], send_sem.at[phase])
        wait_bytes(r_ref.at[rest], recv_sem.at[phase])

    def plane_one(quad, carry):
        store_quad(b_ref, quad, dot_nt(d1_ref[...], v_ref[:, columns(quad)]))
        return carry

    lax.fori_loop(0, 16, plane_one, 0)
    pl.semaphore_wait(barrier, DEVICES - 1)
    stage_y(b_ref, d2_ref, s1, dp % 4, sender(s1, r1, 0))
    load_raw.wait()
    turn_weights(raw_ref, eye_ref, w_ref)
    load_cot.wait()
    arrived(s1, r1, 0)

    line_forward(r1, fwd_ref, x_ref)
    mix(x_ref, w_ref, p_ref)
    line_inverse(p_ref, inv_ref, s2, dp // 2, sender(s2, r2, 1))
    arrived(s2, r2, 1)

    unstage_y(r2, d2t_ref, h_ref)
    acc_ref[...] = jnp.zeros_like(acc_ref)
    sum_ref[...] = jnp.zeros_like(sum_ref)

    def point(quad, carry):
        eye = eye_ref[...]
        v = v_ref[:, columns(quad)]
        vt = dot_nt(eye, v).astype(BF)
        pre = dot(d1t_ref[...], load_quad(h_ref, quad)) + dot(vt, kron_ref[...]) + bias_ref[...]
        square = pre * pre
        th = jnp.tanh(ROOT * pre * (1.0 + 0.044715 * square))
        half = 0.5 + 0.5 * th
        out = (pre * half).astype(BF)
        slope = half + 0.5 * pre * (1.0 - th * th) * (ROOT + (3.0 * 0.044715 * ROOT) * square)
        cot = dot_nt(eye, cot_ref[:, columns(quad)])
        g = (cot * slope).astype(BF)
        g_ref[columns(quad), :] = g
        store_quad(b_ref, quad, dot(d1_ref[...], g))
        out_ref[:, columns(quad)] = dot_nt(eye, out).astype(BF)
        return carry

    lax.fori_loop(0, 16, point, 0)
    stage_y(b_ref, d2_ref, s1, dp % 4, sender(s1, r3, 2))
    store_out = pltpu.make_async_copy(out_ref, out_hbm, store_sem.at[0])
    store_out.start()

    def outer(quad, carry):
        g = g_ref[columns(quad), :]
        acc_ref[...] += dot(v_ref[:, columns(quad)], g)
        sum_ref[...] += jnp.sum(g.astype(F32).reshape(32, 8, 256), axis=0)
        return carry

    lax.fori_loop(0, 16, outer, 0)
    acc = acc_ref[...]
    low = low_lanes((64, 128))
    a = acc[:64, :128] + acc[128:192, 128:]
    b = acc[64:128, :128] + acc[192:, 128:]
    part_ref[pl.ds(0, 8)] = jnp.where(low, a + swap(b), 0.0).reshape(8, 8, 128)
    line = jnp.sum(sum_ref[...], axis=0, keepdims=True)
    line = line[:, :128] + line[:, 128:]
    line = line + swap(line)
    part_ref[8] = jnp.broadcast_to(line, (8, 128))
    part_ref[pl.ds(9, 7)] = jnp.zeros((7, 8, 128), F32)

    def along_slab(source, target_ref, at, number):
        def one(step, carry):
            column = (slab + step) % SLAB
            pltpu.make_async_remote_copy(
                src_ref=source(column),
                dst_ref=target_ref.at[at],
                send_sem=small_send.at[number],
                recv_sem=small_recv.at[number],
                device_id=(dp, column),
                device_id_type=MESH,
            ).start()
            return carry

        lax.fori_loop(1, SLAB, one, 0)

    few = pl.ds(0, SLAB - 1)
    along_slab(lambda column: part_ref.at[column], slab_ref, slab, 0)
    arrived(s1, r3, 2)
    wait_bytes(part_ref.at[few], small_send.at[0])
    wait_bytes(slab_ref.at[few], small_recv.at[0])
    slab_ref[slab] = part_ref[slab]
    half_ref[...] = jnp.sum(slab_ref[...], axis=0)

    def along_dp(step, carry):
        pltpu.make_async_remote_copy(
            src_ref=half_ref,
            dst_ref=dp_ref.at[dp],
            send_sem=small_send.at[1],
            recv_sem=small_recv.at[1],
            device_id=((dp + step) % DP, slab),
            device_id_type=MESH,
        ).start()
        return carry

    lax.fori_loop(1, DP, along_dp, 0)

    line_forward(r3, fwd_ref, y_ref)
    mix_back(y_ref, w_ref, p_ref)
    line_inverse(p_ref, inv_ref, s2, dp // 2, sender(s2, r4, 3))

    seven = pl.ds(0, DP - 1)
    wait_bytes(dp_ref.at[seven], small_send.at[1])
    wait_bytes(dp_ref.at[seven], small_recv.at[1])
    dp_ref[dp] = half_ref[...]
    part_ref[slab] = jnp.sum(dp_ref[...], axis=0) * FACTOR
    total_ref[slab] = part_ref[slab]
    along_slab(lambda column: part_ref.at[slab], total_ref, slab, 2)

    weight_gradient(x_ref, y_ref, eye_ref, sg_ref, w_ref)
    store_sg = pltpu.make_async_copy(sg_ref, sg_hbm, store_sem.at[1])
    store_sg.start()
    wait_bytes(part_ref.at[few], small_send.at[2])
    wait_bytes(total_ref.at[few], small_recv.at[2])
    skip_ref[...] = total_ref[pl.ds(0, 8)].reshape(64, 128)[:, :64]
    line_ref[...] = total_ref[8][:1, :64]
    arrived(s2, r4, 3)

    unstage_y(r4, d2t_ref, h_ref)

    def last(quad, carry):
        value = dot(d1t_ref[...], load_quad(h_ref, quad)) + dot(g_ref[columns(quad), :], kron_back_ref[...])
        back_ref[:, columns(quad)] = dot_nt(eye_ref[...], value.astype(BF)).astype(BF)
        return carry

    lax.fori_loop(0, 16, last, 0)
    store_out.wait()
    store_sg.wait()


WHOLE = pl.BlockSpec(memory_space=pltpu.VMEM)
AWAY = pl.BlockSpec(memory_space=pl.ANY)


def shards(field, cotangent, spectral, skip, bias):
    d1, d1t, d2, d2t, fwd, inv, eye = (jnp.asarray(a) for a in tables())
    shape = lambda dims, dtype: jax.ShapeDtypeStruct(dims, dtype)
    v = jnp.transpose(field[0], (1, 0, 2)).reshape(256, N * N)
    cot = jnp.transpose(cotangent[0], (1, 0, 2)).reshape(256, N * N)
    unit = jnp.eye(4, dtype=BF)
    kron = jnp.einsum("xy,io->xiyo", unit, skip).reshape(256, 256)
    kron_back = jnp.einsum("xy,io->xoyi", unit, skip).reshape(256, 256)
    bias_row = jnp.tile(bias, 4).reshape(1, 256)
    half = pltpu.VMEM((4, 1024, 256), BF)
    grid = pltpu.VMEM((256, N * N), BF)
    modes = pltpu.VMEM((2048, 128), F32)
    weights = pltpu.VMEM((2, C, C, 256), BF)
    chunks = pltpu.VMEM((DEVICES, 32, 128), BF)
    small = lambda count: pltpu.VMEM((count, 8, 128), F32)
    dma = pltpu.SemaphoreType.DMA
    out, back, spectral_grad, skip_grad, bias_grad = pl.pallas_call(
        layer,
        out_shape=(
            shape((256, N * N), BF),
            shape((256, N * N), BF),
            shape((2, C, C, 256), BF),
            shape((C, C), F32),
            shape((1, C), F32),
        ),
        in_specs=[WHOLE, AWAY, AWAY] + [WHOLE] * 10,
        out_specs=[AWAY, WHOLE, AWAY, WHOLE, WHOLE],
        scratch_shapes=[
            grid, weights, grid, weights, pltpu.VMEM((N * N, 256), BF), half, half,
            pltpu.VMEM((256 * 64, 128), F32), modes, modes, modes,
            pltpu.VMEM((256, 256), F32), pltpu.VMEM((8, 256), F32),
            small(16), small(16), pltpu.VMEM((8, 128), F32), small(8), small(16),
        ]
        + [chunks] * 6
        + [dma((4,)), dma((4,)), dma((4,)), dma((2,)), dma((2,)), dma((3,)), dma((3,))],
        compiler_params=pltpu.CompilerParams(
            collective_id=1, has_side_effects=True, vmem_limit_bytes=VMEM_LIMIT
        ),
        name="layer",
    )(v, cot, spectral, kron, kron_back, bias_row, d1, d1t, d2, d2t, fwd, inv, eye)
    spread = lambda a: jnp.transpose(a.reshape(4, C, N * N), (1, 0, 2))[None]
    return (spread(out), spread(back), spectral_grad, skip_grad, bias_grad[0])


def solution(mesh):
    whole = P("dp", None, "slab", None)
    modes = P(None, None, None, ("slab", "dp"))
    return jax.shard_map(
        shards,
        mesh=mesh,
        in_specs=(whole, whole, modes, P(), P()),
        out_specs=(whole, whole, modes, P(), P()),
        check_vma=False,
    )
```

time: 284 us -> 149 us (0.52)
  blocking collectives: 64.3 us -> 0 us
  Pallas kernels: 188 us -> 126 us
  local copies, waits for them, and re-layouts: 29.9 us -> 21.3 us
    psum x1 -> x0, blocking collectives: 64.3 us -> none  [shards(): lax.psum(part[:65, :64], ('dp', 'slab'))]
    pallas_call x10 -> x1, Pallas kernels: 188 us -> 126 us  [shards(): pl.pallas_call(layer, out_shape=(shape((256, N * N), BF), shape((256, N *...]
    reshape x1 -> x0, local copies, waits for them, and re-layouts: 6.55 us -> none  [shards(): w = jnp.transpose(spectral, (3, 1, 0, 2)).reshape(256, C, 2 * C)]
where the time goes in v2:
time: 149 us; the launch traced here: 148 us
  Pallas kernels  126 us (85%)
  local copies, waits for them, and re-layouts  21.3 us (14%)
    pallas_call x1, Pallas kernels, shards(): pl.pallas_call(layer, out_shape=(shape((256, N * N), BF), shape((256, N *...  126 us
    broadcast_in_dim x1, local copies, waits for them, and re-layouts, shards(): spread = lambda a: jnp.transpose(a.reshape(4, C, N * N), (1, 0, 2))[None]  7.36 us
    transpose x1, local copies, waits for them, and re-layouts, shards(): v = jnp.transpose(field[0], (1, 0, 2)).reshape(256, N * N)  4.21 us
    unnamed x12, local copies, waits for them, and re-layouts  3.96 us

profile of v2, /device:TPU:1, one launch (start us, length us, event | category | flops | bytes accessed | tf_op | source)
XLA Modules:
  0.0 148.3 jit_solution(9339926352531346757)
XLA Ops:
  0.6 0.7 tile.2
  1.3 0.6 reshape_tile.3.bias_ref
  1.9 0.8 copy.19
  2.7 0.2 multiply_bitcast_fusion
  3.0 0.9 reshape.32.kron_back_ref
  3.8 0.2 copy.20
  4.1 0.9 reshape.31.kron_ref
  4.9 0.0 copy-start.1
  4.9 4.2 %copy.17 = bf16[4,64,4096]{2,1,0:T(8,128)(2,1)} copy(bf16[4,64,4096]{2,0,1:T(4,128)(2,1)} %bitcast.25) | data formatting | bytes 4194304 | tf_op jit(solution)/shard_map/transpose | solution.py:443
  9.1 0.0 copy-done.1
  9.1 2.5 %copy.18 = bf16[4,64,4096]{2,1,0:T(8,128)(2,1)} copy(bf16[4,64,4096]{2,0,1:T(4,128)(2,1)S(1)} %bitcast.26) | data formatting | bytes 4194304 | tf_op jit(solution)/shard_map/transpose | solution.py:444
  11.6 126.2 %layer.1 = (bf16[256,4096]{1,0:T(8,128)(2,1)}, bf16[256,4096]{1,0:T(8,128)(2,1)}, bf16[2,64,64,256]{3,2,1,0:T(8,128)(2,1)}, f32[64,64]{1,0:T(8,128)}, f32[1,64]{1,0:T(1,128)}) custom-call(bf16[256,4096]{1,0:T(8,128)(2,1)} %bitcast.23, bf16[256,4096]{1,0:T(8,128)(2,1)} %bitcast.24, bf16[2,64,64,256]{3,2,1,0:T(8,128)(2,1)} %raw_hbm.1, ...), custom_call_target="tpu_custom_call" | custom-call | tf_op jit(solution)/shard_map/layer/pallas_call | solution.py:456
  137.8 0.0 copy-start
  137.8 7.4 %copy_bitcast_fusion = (bf16[1,64,4,4096]{3,2,1,0:T(4,128)(2,1)}, bf16[1,64,4,4096]{3,2,1,0:T(4,128)(2,1)}) fusion(bf16[4,64,4096]{2,1,0:T(8,128)(2,1)} %bitcast.28, bf16[4,64,4096]{2,1,0:T(8,128)(2,1)} %bitcast.27), kind=kLoop, calls=%fused_computation | loop fusion | bytes 8388608 | tf_op jit(solution)/shard_map/broadcast_in_dim | solution.py:480
  145.2 0.0 copy-done
  145.2 0.0 copy-start.2
  145.2 0.0 copy-start.3
  145.2 2.0 %copy.28 = bf16[2,64,64,256]{3,2,1,0:T(8,128)(2,1)} copy(bf16[2,64,64,256]{3,2,1,0:T(8,128)(2,1)S(1)} %copy-done) | data formatting | bytes 8388608
  147.2 0.0 copy-done.2
  147.2 0.6 copy.29
  147.8 0.0 copy-done.3
  147.8 0.5 copy.30
  (1 shorter events, 0.0 us)
Async XLA Ops:
  4.9 4.2 %copy-start.1 = (bf16[1,64,4,4096]{3,2,1,0:T(4,128)(2,1)S(1)}, bf16[1,64,4,4096]{3,2,1,0:T(4,128)(2,1)}, u32[]{:S(2)}) copy-start(bf16[1,64,4,4096]{3,2,1,0:T(4,128)(2,1)} %param.13) | copy-start | bytes 6291460
  137.8 7.4 %copy-start = (bf16[2,64,64,256]{3,2,1,0:T(8,128)(2,1)S(1)}, bf16[2,64,64,256]{3,2,1,0:T(8,128)(2,1)}, u32[]{:S(2)}) copy-start(bf16[2,64,64,256]{3,2,1,0:T(8,128)(2,1)} %get-tuple-element.26) | copy-start | bytes 12582916
  145.2 2.0 %copy-start.2 = (f32[64,64]{1,0:T(8,128)S(1)}, f32[64,64]{1,0:T(8,128)}, u32[]{:S(2)}) copy-start(f32[64,64]{1,0:T(8,128)} %get-tuple-element.27) | copy-start | bytes 49156
  145.2 2.6 %copy-start.3 = (f32[1,64]{1,0:T(1,128)S(1)}, f32[1,64]{1,0:T(1,128)}, u32[]{:S(2)}) copy-start(f32[1,64]{1,0:T(1,128)} %get-tuple-element.14) | copy-start | bytes 772

commit v3 on v2

v3 whole, which is shorter than its diff:
```python
import functools
import math

import jax
import jax.numpy as jnp
import ml_dtypes
import numpy as np
from jax import lax
from jax.experimental import pallas as pl
from jax.experimental.pallas import tpu as pltpu
from jax.sharding import PartitionSpec as P

N = 64
M = 32
C = 64
DP = 8
SLAB = 16
DEVICES = DP * SLAB
SAMPLES = 8
BF = jnp.bfloat16
F32 = jnp.float32
MESH = pl.DeviceIdType.MESH
VMEM_LIMIT = 56 * 1024 * 1024


def waves():
    phase = np.mod(np.arange(N)[:, None] * (np.arange(M)[None, :] - M // 2), N)
    angle = phase * (2.0 * math.pi / N)
    return np.cos(angle) / 8.0, np.sin(angle) / 8.0


def tables():
    cos, sin = waves()
    pair = np.stack([cos, -sin], 0).reshape(2, N, 4, 2, 4)
    d1 = np.einsum("tzbhl,uv->hbutlvz", pair, np.eye(4)).reshape(256, 256)
    turn = np.stack([np.stack([cos, sin], 0), np.stack([-sin, cos], 0)], 0)
    turn = turn.reshape(2, 2, N, SLAB, 2)
    d2 = np.einsum("stywx,el->xwseytl", turn, np.eye(4)).reshape(256, 512)
    both = np.stack([cos, sin], 0)
    fwd = np.einsum("axk,ef->aekxf", both, np.eye(4)).reshape(256, 256)
    inv = np.einsum("axk,ef->axefk", both, np.eye(4)).reshape(512, 128)
    eye = np.eye(256)
    order = np.eye(256).reshape(64, 4, 256).transpose(1, 0, 2).reshape(256, 256)
    repeat = np.tile(np.eye(64), (4, 1))
    out = (d1, d1.T, d2, d2.T, fwd, inv, eye, order, order.T, repeat)
    return tuple(np.ascontiguousarray(a).astype(ml_dtypes.bfloat16) for a in out)


def dot(a, b):
    return lax.dot_general(a, b, (((1,), (0,)), ((), ())), preferred_element_type=F32)


def dot_nt(a, b):
    return lax.dot_general(a, b, (((1,), (1,)), ((), ())), preferred_element_type=F32)


def low_lanes(shape):
    return lax.broadcasted_iota(jnp.int32, shape, len(shape) - 1) < 64


def swap(v):
    return pltpu.roll(v, 64, v.ndim - 1)


def signed_swap(v, low_sign):
    turned = swap(v)
    low = low_lanes(v.shape)
    return jnp.where(low, turned, -turned) if low_sign > 0 else jnp.where(low, -turned, turned)


def cross(v):
    upper = lax.broadcasted_iota(jnp.int32, v.shape, v.ndim - 2) < 4
    keep = upper == low_lanes(v.shape)
    return jnp.where(keep, v, swap(pltpu.roll(v, 4, v.ndim - 2)))


def rows_apart(w):
    w = w.reshape(32, 2, 8, 128)
    even, odd = w[:, 0], w[:, 1]
    upper = lax.broadcasted_iota(jnp.int32, even.shape, 1) < 4
    first = jnp.where(upper, even, pltpu.roll(odd, 4, 1))
    second = jnp.where(upper, pltpu.roll(even, 4, 1), odd)
    return jnp.concatenate([first.reshape(256, 128), second.reshape(256, 128)], 1)


def rows_together(value):
    first = value[:, :128].reshape(32, 8, 128)
    second = value[:, 128:].reshape(32, 8, 128)
    upper = lax.broadcasted_iota(jnp.int32, first.shape, 1) < 4
    even = jnp.where(upper, first, pltpu.roll(second, 4, 1))
    odd = jnp.where(upper, pltpu.roll(first, 4, 1), second)
    return jnp.stack([even, odd], 1).reshape(64, 8, 128)


def sixteen(index):
    return pl.ds(pl.multiple_of(index * 16, 16), 16)


def stage_y(b_ref, d2_ref, s_ref, half):
    def one(lb, carry):
        f = dot(d2_ref[...], b_ref[half * 4 + lb]).reshape(32, 8, 256)
        chunk = jnp.concatenate([cross(f[:, :, :128]), cross(f[:, :, 128:])], 1).astype(BF)
        s_ref[half, pl.ds(lb * 16, 16)] = chunk[:16]
        s_ref[half, pl.ds(lb * 16 + 64, 16)] = chunk[16:]
        return carry

    lax.fori_loop(0, 4, one, 0, unroll=True)


def unstage_y(r_ref, d2t_ref, h_ref, half):
    def one(lb, carry):
        r = jnp.concatenate(
            [r_ref[half, pl.ds(lb * 16, 16)], r_ref[half, pl.ds(lb * 16 + 64, 16)]], 0
        ).astype(F32)
        rows = jnp.concatenate([cross(r[:, :8]), cross(r[:, 8:])], 2).reshape(256, 256)
        h_ref[half * 4 + lb] = dot(d2t_ref[...], rows.astype(BF)).astype(BF)
        return carry

    lax.fori_loop(0, 4, one, 0, unroll=True)


def store_quad(b_ref, quad, value):
    b_ref[:, pl.ds(pl.multiple_of(quad * 32, 32), 32), :] = value.astype(BF).reshape(8, 32, 256)


def load_quad(h_ref, quad):
    return h_ref[:, pl.ds(pl.multiple_of(quad * 32, 32), 32), :].reshape(256, 256)


def columns(quad):
    return pl.ds(pl.multiple_of(quad * 256, 256), 256)


def line_forward(r_ref, fwd_ref, x_ref, half):
    def one(pair, carry):
        a = r_ref[half, pl.ds(32 * pair, 16)].reshape(256, 128)
        b = r_ref[half, pl.ds(32 * pair + 16, 16)].reshape(256, 128)
        y = dot(fwd_ref[...], jnp.concatenate([a, b], 1))
        for h in range(2):
            lanes = slice(128 * h, 128 * h + 128)
            modes = y[:128, lanes] + signed_swap(y[128:, lanes], 1)
            x_ref[pl.ds(1024 * half + 2 * pair + h, 128, stride=8), :] = modes.astype(BF).astype(F32)
        return carry

    lax.fori_loop(0, 4, one, 0, unroll=True)


def line_inverse(p_ref, inv_ref, s_ref, half):
    def one(pair, carry):
        a = p_ref[pl.ds(1024 * half + 2 * pair, 128, stride=8), :].astype(BF)
        b = p_ref[pl.ds(1024 * half + 2 * pair + 1, 128, stride=8), :].astype(BF)
        y = dot(inv_ref[...], jnp.concatenate([a, b], 1))
        for h in range(2):
            lanes = slice(128 * h, 128 * h + 128)
            lines = y[:256, lanes] + signed_swap(y[256:, lanes], -1)
            s_ref[half, pl.ds(32 * pair + 16 * h, 16)] = lines.astype(BF).reshape(16, 16, 128)
        return carry

    lax.fori_loop(0, 4, one, 0, unroll=True)


def mix(x_ref, w_ref, p_ref, half):
    row_mode = lax.broadcasted_iota(jnp.int32, (32, 128), 0) // 8
    low = low_lanes((32, 128))

    def one(group, carry):
        x = x_ref[pl.ds(pl.multiple_of(group * 32, 32), 32), :]
        xs = swap(x)
        zero = jnp.zeros_like(x)
        top, bottom = [], []
        for h in range(2):
            even = jnp.logical_and(row_mode == 2 * h, low)
            odd = jnp.logical_and(row_mode == 2 * h + 1, jnp.logical_not(low))
            top.append(jnp.where(even, x, jnp.where(odd, xs, zero)))
            bottom.append(jnp.where(even, xs, jnp.where(odd, x, zero)))
        left = jnp.concatenate(
            [jnp.concatenate(top, 1), jnp.concatenate(bottom, 1)], 0
        ).astype(BF)
        w = w_ref[pl.ds(pl.multiple_of(group * 256, 256), 256), :].astype(BF)
        z = dot(left, w)
        p_ref[pl.ds(pl.multiple_of(group * 32, 32), 32), :] = z[:32] + signed_swap(z[32:], -1)
        return carry

    lax.fori_loop(32 * half, 32 * half + 32, one, 0, unroll=4)


def mix_back(g_ref, w_ref, p_ref, half):
    row_mode = lax.broadcasted_iota(jnp.int32, (32, 128), 0) // 8
    low = low_lanes((32, 128))

    def one(group, carry):
        g = g_ref[pl.ds(pl.multiple_of(group * 32, 32), 32), :]
        left = jnp.concatenate([g, signed_swap(g, 1)], 0).astype(BF)
        w = w_ref[pl.ds(pl.multiple_of(group * 256, 256), 256), :].astype(BF)
        z = dot_nt(left, w)
        z0, z1 = z[:32], z[32:]
        even = row_mode % 2 == 0
        first = row_mode < 2
        a0 = jnp.where(first, z0[:, :128], z0[:, 128:])
        a1 = jnp.where(first, z1[:, :128], z1[:, 128:])
        b0 = jnp.where(even, a0, swap(a0))
        b1 = jnp.where(even, swap(a1), a1)
        p_ref[pl.ds(pl.multiple_of(group * 32, 32), 32), :] = jnp.where(low, b0, b1)
        return carry

    lax.fori_loop(32 * half, 32 * half + 32, one, 0, unroll=4)


ROOT = math.sqrt(2.0 / math.pi)
FACTOR = 1.0 / math.sqrt(SAMPLES * N * N * N)


def turn_weights(raw_ref, eye_ref, w_ref, half):
    lanes = slice(128 * half, 128 * half + 128)

    def one(i, carry):
        plane = jnp.concatenate([raw_ref[0, i, :, lanes], raw_ref[1, i, :, lanes]], 0)
        turned = dot_nt(eye_ref[pl.ds(0, 128), pl.ds(0, 128)], plane)
        w_ref[pl.ds(8192 * half + i, 128, stride=64), :] = turned
        return carry

    lax.fori_loop(0, 64, one, 0, unroll=4)


def weight_gradient(x_ref, g_ref, eye_ref, out_ref, a_ref):
    lane_mode = (lax.broadcasted_iota(jnp.int32, (64, 256), 1) // 8) % 16

    def one(group, carry):
        rows = pl.ds(pl.multiple_of(group * 128, 128), 128)
        xt = x_ref[rows, :].T
        xt = jnp.concatenate([xt[:64], xt[64:]], 1)
        g = g_ref[rows, :]
        right = jnp.concatenate([g, signed_swap(g, 1)], 0).astype(BF)
        left = jnp.concatenate(
            [jnp.where(lane_mode == m, xt, 0.0) for m in range(16)], 0
        ).astype(BF)
        a_ref[pl.ds(pl.multiple_of(group * 1024, 1024), 1024), :] = dot(left, right)
        return carry

    lax.fori_loop(0, 16, one, 0)

    def turn(i, carry):
        value = a_ref[pl.ds(i, 256, stride=64), :].astype(BF)
        plane = dot_nt(eye_ref[pl.ds(0, 128), pl.ds(0, 128)], value).astype(BF)
        out_ref[0, i] = plane[:64]
        out_ref[1, i] = plane[64:]
        return carry

    lax.fori_loop(0, 64, turn, 0, unroll=2)


def layer(
    field_hbm, cot_hbm, raw_hbm, skip_in, bias_in,
    d1_ref, d1t_ref, d2_ref, d2t_ref, fwd_ref, inv_ref, eye_ref, order_ref, back_order_ref, repeat_ref,
    out_hbm, back_hbm, sg_hbm, skip_ref, line_ref,
    io_ref, cot_ref, raw_ref, v_ref, ct_ref, out_ref, g_ref, vk_ref, h_ref, b_ref, w_ref,
    x_ref, y_ref, p_ref, kron_ref,
    acc_ref, sum_ref, part_ref, slab_ref, half_ref, dp_ref, total_ref,
    s1, s2, r1, r2, r3, r4,
    send_sem, recv_sem, local_sem, load_sem, store_sem, small_send, small_recv,
):
    dp = lax.axis_index("dp")
    slab = lax.axis_index("slab")
    me = dp * SLAB + slab

    def wait_bytes(ref, sem):
        pltpu.make_async_copy(ref, ref, sem).wait()

    def partner(i):
        step = (i * 37) % DEVICES
        return (dp + step // SLAB) % DP, (slab + step % SLAB) % SLAB

    barrier = pltpu.get_barrier_semaphore()
    load_field = pltpu.make_async_copy(field_hbm, io_ref, load_sem.at[0])
    load_raw = pltpu.make_async_copy(raw_hbm, raw_ref, load_sem.at[1])
    load_cot = pltpu.make_async_copy(cot_hbm, cot_ref, load_sem.at[2])
    load_field.start()
    load_raw.start()
    load_cot.start()

    def greet(i, carry):
        pl.semaphore_signal(barrier, inc=1, device_id=partner(i), device_id_type=MESH)
        return carry

    lax.fori_loop(1, DEVICES, greet, 0)

    rest = pl.ds(0, DEVICES - 1)

    def send(s_ref, r_ref, phase, half):
        at = 2 * phase + half
        pltpu.make_async_copy(s_ref.at[half, me], r_ref.at[half, me], local_sem.at[at]).start()

        def one(i, carry):
            to = partner(i)
            pltpu.make_async_remote_copy(
                src_ref=s_ref.at[half, to[0] * SLAB + to[1]],
                dst_ref=r_ref.at[half, me],
                send_sem=send_sem.at[at],
                recv_sem=recv_sem.at[at],
                device_id=to,
                device_id_type=MESH,
            ).start()
            return carry

        lax.fori_loop(1, DEVICES, one, 0)

    def arrived(s_ref, r_ref, phase, half):
        at = 2 * phase + half
        pltpu.make_async_copy(s_ref.at[half, me], r_ref.at[half, me], local_sem.at[at]).wait()
        wait_bytes(r_ref.at[half, rest], recv_sem.at[at])

    def sent(s_ref, phase):
        for half in range(2):
            wait_bytes(s_ref.at[half, rest], send_sem.at[2 * phase + half])

    wide = dot_nt(dot(repeat_ref[...], skip_in[...]).astype(BF), repeat_ref[...])
    same = (
        lax.broadcasted_iota(jnp.int32, (256, 256), 0) // 64
        == lax.broadcasted_iota(jnp.int32, (256, 256), 1) // 64
    )
    kron_ref[...] = jnp.where(same, wide, 0.0).astype(BF)
    bias = jnp.concatenate([bias_in[...]] * 4, 1)

    load_field.wait()

    def plane_one(index, carry):
        block = io_ref[:, sixteen(index), :].astype(F32)
        for j in range(2):
            v = rows_apart(block[:, 8 * j : 8 * j + 8]).astype(BF)
            v = dot(order_ref[...], v).astype(BF)
            v_ref[:, columns(2 * index + j)] = v
            store_quad(b_ref, 2 * index + j, dot_nt(d1_ref[...], v))
        return carry

    lax.fori_loop(0, 8, plane_one, 0)
    stage_y(b_ref, d2_ref, s1, 0)
    pl.semaphore_wait(barrier, DEVICES - 1)
    send(s1, r1, 0, 0)
    stage_y(b_ref, d2_ref, s1, 1)
    send(s1, r1, 0, 1)
    load_raw.wait()

    for half in range(2):
        turn_weights(raw_ref, eye_ref, w_ref, half)
        arrived(s1, r1, 0, half)
        line_forward(r1, fwd_ref, x_ref, half)
        mix(x_ref, w_ref, p_ref, half)
        line_inverse(p_ref, inv_ref, s2, half)
        send(s2, r2, 1, half)

    load_cot.wait()

    def prepare(index, carry):
        block = cot_ref[:, sixteen(index), :].astype(F32)
        for j in range(2):
            quad = columns(2 * index + j)
            cot = rows_apart(block[:, 8 * j : 8 * j + 8]).astype(BF)
            cot = dot(order_ref[...], cot).astype(BF)
            ct_ref[quad, :] = dot_nt(eye_ref[...], cot).astype(BF)
            vt = dot_nt(eye_ref[...], v_ref[:, quad]).astype(BF)
            vk_ref[quad, :] = dot(vt, kron_ref[...]) + bias
        return carry

    lax.fori_loop(0, 8, prepare, 0)
    for half in range(2):
        arrived(s2, r2, 1, half)
        unstage_y(r2, d2t_ref, h_ref, half)

    def point(index, carry):
        for j in range(2):
            quad = 2 * index + j
            pre = dot(d1t_ref[...], load_quad(h_ref, quad)) + vk_ref[columns(quad), :]
            square = pre * pre
            th = jnp.tanh(ROOT * pre * (1.0 + 0.044715 * square))
            half = 0.5 + 0.5 * th
            out_ref[columns(quad), :] = (pre * half).astype(BF)
            slope = half + 0.5 * pre * (1.0 - th * th) * (ROOT + (3.0 * 0.044715 * ROOT) * square)
            g = (ct_ref[columns(quad), :].astype(F32) * slope).astype(BF)
            g_ref[columns(quad), :] = g
            store_quad(b_ref, quad, dot(d1_ref[...], g))
        return carry

    lax.fori_loop(0, 8, point, 0)
    sent(s1, 0)
    for half in range(2):
        stage_y(b_ref, d2_ref, s1, half)
        send(s1, r3, 2, half)

    acc_ref[...] = jnp.zeros_like(acc_ref)
    sum_ref[...] = jnp.zeros_like(sum_ref)

    def outer(quad, carry):
        g = g_ref[columns(quad), :]
        acc_ref[...] += dot(v_ref[:, columns(quad)], g)
        sum_ref[...] += jnp.sum(g.astype(F32).reshape(32, 8, 256), axis=0)
        return carry

    lax.fori_loop(0, 16, outer, 0, unroll=2)
    acc = acc_ref[...]
    low = low_lanes((64, 128))
    a = acc[:64, :128] + acc[128:192, 128:]
    b = acc[64:128, :128] + acc[192:, 128:]
    part_ref[pl.ds(0, 8)] = jnp.where(low, a + swap(b), 0.0).reshape(8, 8, 128)
    line = jnp.sum(sum_ref[...], axis=0, keepdims=True)
    line = line[:, :128] + line[:, 128:]
    line = line + swap(line)
    part_ref[8] = jnp.broadcast_to(line, (8, 128))
    part_ref[pl.ds(9, 7)] = jnp.zeros((7, 8, 128), F32)

    def along_slab(source, target_ref, at, number):
        def one(step, carry):
            column = (slab + step) % SLAB
            pltpu.make_async_remote_copy(
                src_ref=source(column),
                dst_ref=target_ref.at[at],
                send_sem=small_send.at[number],
                recv_sem=small_recv.at[number],
                device_id=(dp, column),
                device_id_type=MESH,
            ).start()
            return carry

        lax.fori_loop(1, SLAB, one, 0)

    few = pl.ds(0, SLAB - 1)
    along_slab(lambda column: part_ref.at[column], slab_ref, slab, 0)

    def turn_out(index, carry):
        both = []
        for j in range(2):
            both.append(rows_together(dot_nt(back_order_ref[...], out_ref[columns(2 * index + j), :])))
        io_ref[:, sixteen(index), :] = jnp.concatenate(both, 1).astype(BF)
        return carry

    lax.fori_loop(0, 8, turn_out, 0)
    store_out = pltpu.make_async_copy(io_ref, out_hbm, store_sem.at[0])
    store_out.start()

    sent(s2, 1)
    for half in range(2):
        arrived(s1, r3, 2, half)
        line_forward(r3, fwd_ref, y_ref, half)
        mix_back(y_ref, w_ref, p_ref, half)
        line_inverse(p_ref, inv_ref, s2, half)
        send(s2, r4, 3, half)

    wait_bytes(part_ref.at[few], small_send.at[0])
    wait_bytes(slab_ref.at[few], small_recv.at[0])
    slab_ref[slab] = part_ref[slab]
    half_ref[...] = jnp.sum(slab_ref[...], axis=0)

    def along_dp(step, carry):
        pltpu.make_async_remote_copy(
            src_ref=half_ref,
            dst_ref=dp_ref.at[dp],
            send_sem=small_send.at[1],
            recv_sem=small_recv.at[1],
            device_id=((dp + step) % DP, slab),
            device_id_type=MESH,
        ).start()
        return carry

    lax.fori_loop(1, DP, along_dp, 0)
    weight_gradient(x_ref, y_ref, eye_ref, raw_ref, w_ref)
    store_sg = pltpu.make_async_copy(raw_ref, sg_hbm, store_sem.at[1])
    store_sg.start()

    seven = pl.ds(0, DP - 1)
    wait_bytes(dp_ref.at[seven], small_send.at[1])
    wait_bytes(dp_ref.at[seven], small_recv.at[1])
    dp_ref[dp] = half_ref[...]
    part_ref[slab] = jnp.sum(dp_ref[...], axis=0) * FACTOR
    total_ref[slab] = part_ref[slab]
    along_slab(lambda column: part_ref.at[slab], total_ref, slab, 2)

    def skip_back(quad, carry):
        vk_ref[columns(quad), :] = dot_nt(g_ref[columns(quad), :], kron_ref[...])
        return carry

    lax.fori_loop(0, 16, skip_back, 0, unroll=2)
    for half in range(2):
        arrived(s2, r4, 3, half)
        unstage_y(r4, d2t_ref, h_ref, half)

    def last(index, carry):
        both = []
        for j in range(2):
            quad = 2 * index + j
            value = dot(d1t_ref[...], load_quad(h_ref, quad)) + vk_ref[columns(quad), :]
            both.append(rows_together(dot_nt(back_order_ref[...], value.astype(BF))))
        cot_ref[:, sixteen(index), :] = jnp.concatenate(both, 1).astype(BF)
        return carry

    lax.fori_loop(0, 8, last, 0)
    store_back = pltpu.make_async_copy(cot_ref, back_hbm, store_sem.at[2])
    store_back.start()
    sent(s1, 2)
    sent(s2, 3)
    wait_bytes(part_ref.at[few], small_send.at[2])
    wait_bytes(total_ref.at[few], small_recv.at[2])
    skip_ref[...] = total_ref[pl.ds(0, 8)].reshape(64, 128)[:, :64]
    line_ref[...] = total_ref[8][:1, :64]
    store_out.wait()
    store_sg.wait()
    store_back.wait()


WHOLE = pl.BlockSpec(memory_space=pltpu.VMEM)
AWAY = pl.BlockSpec(memory_space=pl.ANY)


def shards(field, cotangent, spectral, skip, bias):
    constants = tuple(jnp.asarray(a) for a in tables())
    shape = lambda dims, dtype: jax.ShapeDtypeStruct(dims, dtype)

    def gather(a):
        return jnp.transpose(a.reshape(C, 4, 32, 128), (0, 2, 1, 3)).reshape(C, 128, 128)

    def spread(a):
        return jnp.transpose(a.reshape(C, 32, 4, 128), (0, 2, 1, 3)).reshape(1, C, 4, N * N)

    grid = pltpu.VMEM((256, N * N), BF)
    turned = pltpu.VMEM((N * N, 256), BF)
    block = pltpu.VMEM((C, 128, 128), BF)
    planes = pltpu.VMEM((8, 512, 256), BF)
    modes = pltpu.VMEM((2048, 128), F32)
    chunks = pltpu.VMEM((2, DEVICES, 16, 128), BF)
    small = lambda count: pltpu.VMEM((count, 8, 128), F32)
    dma = pltpu.SemaphoreType.DMA
    out, back, spectral_grad, skip_grad, bias_grad = pl.pallas_call(
        layer,
        out_shape=(
            shape((C, 128, 128), BF),
            shape((C, 128, 128), BF),
            shape((2, C, C, 256), BF),
            shape((C, C), F32),
            shape((1, C), F32),
        ),
        in_specs=[AWAY, AWAY, AWAY] + [WHOLE] * 12,
        out_specs=[AWAY, AWAY, AWAY, WHOLE, WHOLE],
        scratch_shapes=[
            block, block, pltpu.VMEM((2, C, C, 256), BF), grid, turned, turned, turned,
            pltpu.VMEM((N * N, 256), F32), planes, planes, pltpu.VMEM((256 * 64, 128), F32),
            modes, modes, modes, pltpu.VMEM((256, 256), BF),
            pltpu.VMEM((256, 256), F32), pltpu.VMEM((8, 256), F32),
            small(16), small(16), pltpu.VMEM((8, 128), F32), small(8), small(16),
        ]
        + [chunks] * 6
        + [dma((8,)), dma((8,)), dma((8,)), dma((3,)), dma((3,)), dma((3,)), dma((3,))],
        compiler_params=pltpu.CompilerParams(
            collective_id=1, has_side_effects=True, vmem_limit_bytes=VMEM_LIMIT
        ),
        name="layer",
    )(gather(field), gather(cotangent), spectral, skip, bias.reshape(1, C), *constants)
    return (spread(out), spread(back), spectral_grad, skip_grad, bias_grad[0])


def solution(mesh):
    whole = P("dp", None, "slab", None)
    modes = P(None, None, None, ("slab", "dp"))
    return jax.shard_map(
        shards,
        mesh=mesh,
        in_specs=(whole, whole, modes, P(), P()),
        out_specs=(whole, whole, modes, P(), P()),
        check_vma=False,
    )
```

time: 149 us -> 122 us (0.82)
  Pallas kernels: 126 us -> 110 us
  local copies, waits for them, and re-layouts: 21.3 us -> 10.7 us
    pallas_call x1, Pallas kernels: 126 us -> 110 us  [shards(): pl.pallas_call(layer, out_shape=(shape((C, 128, 128), BF), shape((C, 128,...]
    broadcast_in_dim x1 -> x0, local copies, waits for them, and re-layouts: 7.36 us -> none  [shards(): spread = lambda a: jnp.transpose(a.reshape(4, C, N * N), (1, 0, 2))[None]]
    transpose x3 -> x0, local copies, waits for them, and re-layouts: 6.89 us -> none  [the longest x1 4.21 us: shards(): v = jnp.transpose(field[0], (1, 0, 2)).reshape(256, N * N)]
    unnamed x12 -> x13, local copies, waits for them, and re-layouts: 3.96 us -> 10.7 us
    reshape x2 -> x0, local copies, waits for them, and re-layouts: 1.74 us -> none  [the longest x1 0.87 us: shards(): kron = jnp.einsum('xy,io->xiyo', unit, skip).reshape(256, 256)]
where the time goes in v3:
time: 122 us; the launch traced here: 121 us
  Pallas kernels  110 us (90%)
  local copies, waits for them, and re-layouts  10.7 us (9%)
    pallas_call x1, Pallas kernels, shards(): pl.pallas_call(layer, out_shape=(shape((C, 128, 128), BF), shape((C, 128,...  110 us
    unnamed x13, local copies, waits for them, and re-layouts  10.7 us

profile of v3, /device:TPU:1, one launch (start us, length us, event | category | flops | bytes accessed | tf_op | source)
XLA Modules:
  0.0 121.4 jit_solution(3866025970994568881)
XLA Ops:
  0.6 110.0 %layer.1 = (bf16[64,128,128]{2,1,0:T(8,128)(2,1)}, bf16[64,128,128]{2,1,0:T(8,128)(2,1)}, bf16[2,64,64,256]{3,2,1,0:T(8,128)(2,1)}, f32[64,64]{1,0:T(8,128)}, f32[1,64]{1,0:T(1,128)}) custom-call(bf16[64,128,128]{2,1,0:T(8,128)(2,1)} %bitcast.22, bf16[64,128,128]{2,1,0:T(8,128)(2,1)} %bitcast.23, bf16[2,64,64,256]{3,2,1,0:T(8,128)(2,1)} %raw_hbm.1, ...), custom_call_target="tpu_custom_call" | custom-call | tf_op jit(solution)/shard_map/layer/pallas_call | solution.py:530
  110.6 0.0 copy-start.1
  110.6 4.6 %copy.29 = bf16[1,64,4,4096]{3,2,1,0:T(4,128)(2,1)} copy(bf16[1,64,4,4096]{3,2,1,0:T(4,128)(2,1)} %bitcast.25) | data formatting | bytes 4194304
  115.3 0.0 copy-done.1
  115.3 0.0 copy-start
  115.3 1.3 %copy.30 = bf16[1,64,4,4096]{3,2,1,0:T(4,128)(2,1)} copy(bf16[1,64,4,4096]{3,2,1,0:T(4,128)(2,1)S(1)} %bitcast.24) | data formatting | bytes 4194304
  116.6 1.6 %copy-done = bf16[2,64,64,256]{3,2,1,0:T(8,128)(2,1)S(1)} copy-done((bf16[2,64,64,256]{3,2,1,0:T(8,128)(2,1)S(1)}, bf16[2,64,64,256]{3,2,1,0:T(8,128)(2,1)}, u32[]{:S(2)}) %copy-start) | copy-done | bytes 4194328
  118.2 0.0 copy-start.2
  118.2 0.0 copy-start.3
  118.2 2.0 %copy.31 = bf16[2,64,64,256]{3,2,1,0:T(8,128)(2,1)} copy(bf16[2,64,64,256]{3,2,1,0:T(8,128)(2,1)S(1)} %copy-done) | data formatting | bytes 8388608
  120.2 0.0 copy-done.2
  120.2 0.6 copy.32
  120.8 0.0 copy-done.3
  120.8 0.5 copy.33
Async XLA Ops:
  110.6 4.6 %copy-start.1 = (bf16[64,128,128]{2,1,0:T(8,128)(2,1)S(1)}, bf16[64,128,128]{2,1,0:T(8,128)(2,1)}, u32[]{:S(2)}) copy-start(bf16[64,128,128]{2,1,0:T(8,128)(2,1)} %get-tuple-element.11) | copy-start | bytes 6291460
  115.3 2.9 %copy-start = (bf16[2,64,64,256]{3,2,1,0:T(8,128)(2,1)S(1)}, bf16[2,64,64,256]{3,2,1,0:T(8,128)(2,1)}, u32[]{:S(2)}) copy-start(bf16[2,64,64,256]{3,2,1,0:T(8,128)(2,1)} %get-tuple-element.22) | copy-start | bytes 12582916
  118.2 2.0 %copy-start.2 = (f32[64,64]{1,0:T(8,128)S(1)}, f32[64,64]{1,0:T(8,128)}, u32[]{:S(2)}) copy-start(f32[64,64]{1,0:T(8,128)} %get-tuple-element.23) | copy-start | bytes 49156
  118.2 2.6 %copy-start.3 = (f32[1,64]{1,0:T(1,128)S(1)}, f32[1,64]{1,0:T(1,128)}, u32[]{:S(2)}) copy-start(f32[1,64]{1,0:T(1,128)} %get-tuple-element.14) | copy-start | bytes 772

commit v4 on v3

--- a/solution.py
+++ b/solution.py
@@ -159,6 +159,14 @@
     lax.fori_loop(0, 4, one, 0, unroll=True)
 
 
+PITCH = 72
+
+
+def four_rows(w_ref, group):
+    first = pl.multiple_of(group * (4 * PITCH), 8)
+    return jnp.concatenate([w_ref[pl.ds(first + PITCH * m, 64), :] for m in range(4)], 0).astype(BF)
+
+
 def mix(x_ref, w_ref, p_ref, half):
     row_mode = lax.broadcasted_iota(jnp.int32, (32, 128), 0) // 8
     low = low_lanes((32, 128))
@@ -176,7 +184,7 @@
         left = jnp.concatenate(
             [jnp.concatenate(top, 1), jnp.concatenate(bottom, 1)], 0
         ).astype(BF)
-        w = w_ref[pl.ds(pl.multiple_of(group * 256, 256), 256), :].astype(BF)
+        w = four_rows(w_ref, group)
         z = dot(left, w)
         p_ref[pl.ds(pl.multiple_of(group * 32, 32), 32), :] = z[:32] + signed_swap(z[32:], -1)
         return carry
@@ -191,7 +199,7 @@
     def one(group, carry):
         g = g_ref[pl.ds(pl.multiple_of(group * 32, 32), 32), :]
         left = jnp.concatenate([g, signed_swap(g, 1)], 0).astype(BF)
-        w = w_ref[pl.ds(pl.multiple_of(group * 256, 256), 256), :].astype(BF)
+        w = four_rows(w_ref, group)
         z = dot_nt(left, w)
         z0, z1 = z[:32], z[32:]
         even = row_mode % 2 == 0
@@ -216,7 +224,7 @@
     def one(i, carry):
         plane = jnp.concatenate([raw_ref[0, i, :, lanes], raw_ref[1, i, :, lanes]], 0)
         turned = dot_nt(eye_ref[pl.ds(0, 128), pl.ds(0, 128)], plane)
-        w_ref[pl.ds(8192 * half + i, 128, stride=64), :] = turned
+        w_ref[pl.ds(128 * PITCH * half + i, 128, stride=PITCH), :] = turned
         return carry
 
     lax.fori_loop(0, 64, one, 0, unroll=4)
@@ -234,19 +242,22 @@
         left = jnp.concatenate(
             [jnp.where(lane_mode == m, xt, 0.0) for m in range(16)], 0
         ).astype(BF)
-        a_ref[pl.ds(pl.multiple_of(group * 1024, 1024), 1024), :] = dot(left, right)
+        value = dot(left, right)
+        first = pl.multiple_of(group * (16 * PITCH), 8)
+        for m in range(16):
+            a_ref[pl.ds(first + PITCH * m, 64), :] = value[64 * m : 64 * m + 64]
         return carry
 
     lax.fori_loop(0, 16, one, 0)
 
     def turn(i, carry):
-        value = a_ref[pl.ds(i, 256, stride=64), :].astype(BF)
+        value = a_ref[pl.ds(i, 256, stride=PITCH), :].astype(BF)
         plane = dot_nt(eye_ref[pl.ds(0, 128), pl.ds(0, 128)], value).astype(BF)
         out_ref[0, i] = plane[:64]
         out_ref[1, i] = plane[64:]
         return carry
 
-    lax.fori_loop(0, 64, turn, 0, unroll=2)
+    lax.fori_loop(0, 64, turn, 0, unroll=4)
 
 
 def layer(
@@ -266,9 +277,20 @@
     def wait_bytes(ref, sem):
         pltpu.make_async_copy(ref, ref, sem).wait()
 
-    def partner(i):
-        step = (i * 37) % DEVICES
-        return (dp + step // SLAB) % DP, (slab + step % SLAB) % SLAB
+    column = [slab] + [lax.rem(slab + step, SLAB) for step in range(1, SLAB)]
+
+    def everybody(act):
+        def one(turn, carry):
+            for step in range(1, SLAB):
+                act(lax.rem(dp + turn + step, DP), column[step])
+            return carry
+
+        def own(turn, carry):
+            act(lax.rem(dp + turn, DP), slab)
+            return carry
+
+        lax.fori_loop(0, DP, one, 0)
+        lax.fori_loop(1, DP, own, 0, unroll=True)
 
     barrier = pltpu.get_barrier_semaphore()
     load_field = pltpu.make_async_copy(field_hbm, io_ref, load_sem.at[0])
@@ -278,11 +300,11 @@
     load_raw.start()
     load_cot.start()
 
-    def greet(i, carry):
-        pl.semaphore_signal(barrier, inc=1, device_id=partner(i), device_id_type=MESH)
-        return carry
-
-    lax.fori_loop(1, DEVICES, greet, 0)
+    everybody(
+        lambda row, place: pl.semaphore_signal(
+            barrier, inc=1, device_id=(row, place), device_id_type=MESH
+        )
+    )
 
     rest = pl.ds(0, DEVICES - 1)
 
@@ -290,19 +312,17 @@
         at = 2 * phase + half
         pltpu.make_async_copy(s_ref.at[half, me], r_ref.at[half, me], local_sem.at[at]).start()
 
-        def one(i, carry):
-            to = partner(i)
+        def one(row, place):
             pltpu.make_async_remote_copy(
-                src_ref=s_ref.at[half, to[0] * SLAB + to[1]],
+                src_ref=s_ref.at[half, row * SLAB + place],
                 dst_ref=r_ref.at[half, me],
                 send_sem=send_sem.at[at],
                 recv_sem=recv_sem.at[at],
-                device_id=to,
+                device_id=(row, place),
                 device_id_type=MESH,
             ).start()
-            return carry
-
-        lax.fori_loop(1, DEVICES, one, 0)
+
+        everybody(one)
 
     def arrived(s_ref, r_ref, phase, half):
         at = 2 * phase + half
@@ -332,7 +352,7 @@
             store_quad(b_ref, 2 * index + j, dot_nt(d1_ref[...], v))
         return carry
 
-    lax.fori_loop(0, 8, plane_one, 0)
+    lax.fori_loop(0, 8, plane_one, 0, unroll=2)
     stage_y(b_ref, d2_ref, s1, 0)
     pl.semaphore_wait(barrier, DEVICES - 1)
     send(s1, r1, 0, 0)
@@ -361,7 +381,7 @@
             vk_ref[quad, :] = dot(vt, kron_ref[...]) + bias
         return carry
 
-    lax.fori_loop(0, 8, prepare, 0)
+    lax.fori_loop(0, 8, prepare, 0, unroll=2)
     for half in range(2):
         arrived(s2, r2, 1, half)
         unstage_y(r2, d2t_ref, h_ref, half)
@@ -371,16 +391,16 @@
             quad = 2 * index + j
             pre = dot(d1t_ref[...], load_quad(h_ref, quad)) + vk_ref[columns(quad), :]
             square = pre * pre
-            th = jnp.tanh(ROOT * pre * (1.0 + 0.044715 * square))
-            half = 0.5 + 0.5 * th
-            out_ref[columns(quad), :] = (pre * half).astype(BF)
-            slope = half + 0.5 * pre * (1.0 - th * th) * (ROOT + (3.0 * 0.044715 * ROOT) * square)
+            half = 0.5 + 0.5 * jnp.tanh(pre * (ROOT + (ROOT * 0.044715) * square))
+            out = pre * half
+            out_ref[columns(quad), :] = out.astype(BF)
+            slope = half + out * (1.0 - half) * (2.0 * ROOT + (6.0 * 0.044715 * ROOT) * square)
             g = (ct_ref[columns(quad), :].astype(F32) * slope).astype(BF)
             g_ref[columns(quad), :] = g
             store_quad(b_ref, quad, dot(d1_ref[...], g))
         return carry
 
-    lax.fori_loop(0, 8, point, 0)
+    lax.fori_loop(0, 8, point, 0, unroll=2)
     sent(s1, 0)
     for half in range(2):
         stage_y(b_ref, d2_ref, s1, half)
@@ -408,22 +428,18 @@
     part_ref[pl.ds(9, 7)] = jnp.zeros((7, 8, 128), F32)
 
     def along_slab(source, target_ref, at, number):
-        def one(step, carry):
-            column = (slab + step) % SLAB
+        for step in range(1, SLAB):
             pltpu.make_async_remote_copy(
-                src_ref=source(column),
+                src_ref=source(column[step]),
                 dst_ref=target_ref.at[at],
                 send_sem=small_send.at[number],
                 recv_sem=small_recv.at[number],
-                device_id=(dp, column),
+                device_id=(dp, column[step]),
                 device_id_type=MESH,
             ).start()
-            return carry
-
-        lax.fori_loop(1, SLAB, one, 0)
 
     few = pl.ds(0, SLAB - 1)
-    along_slab(lambda column: part_ref.at[column], slab_ref, slab, 0)
+    along_slab(lambda place: part_ref.at[place], slab_ref, slab, 0)
 
     def turn_out(index, carry):
         both = []
@@ -432,9 +448,15 @@
         io_ref[:, sixteen(index), :] = jnp.concatenate(both, 1).astype(BF)
         return carry
 
-    lax.fori_loop(0, 8, turn_out, 0)
+    lax.fori_loop(0, 8, turn_out, 0, unroll=2)
     store_out = pltpu.make_async_copy(io_ref, out_hbm, store_sem.at[0])
     store_out.start()
+
+    def skip_back(quad, carry):
+        vk_ref[columns(quad), :] = dot_nt(g_ref[columns(quad), :], kron_ref[...])
+        return carry
+
+    lax.fori_loop(0, 16, skip_back, 0, unroll=2)
 
     sent(s2, 1)
     for half in range(2):
@@ -455,7 +477,7 @@
             dst_ref=dp_ref.at[dp],
             send_sem=small_send.at[1],
             recv_sem=small_recv.at[1],
-            device_id=((dp + step) % DP, slab),
+            device_id=(lax.rem(dp + step, DP), slab),
             device_id_type=MESH,
         ).start()
         return carry
@@ -471,13 +493,8 @@
     dp_ref[dp] = half_ref[...]
     part_ref[slab] = jnp.sum(dp_ref[...], axis=0) * FACTOR
     total_ref[slab] = part_ref[slab]
-    along_slab(lambda column: part_ref.at[slab], total_ref, slab, 2)
-
-    def skip_back(quad, carry):
-        vk_ref[columns(quad), :] = dot_nt(g_ref[columns(quad), :], kron_ref[...])
-        return carry
-
-    lax.fori_loop(0, 16, skip_back, 0, unroll=2)
+    along_slab(lambda place: part_ref.at[slab], total_ref, slab, 2)
+
     for half in range(2):
         arrived(s2, r4, 3, half)
         unstage_y(r4, d2t_ref, h_ref, half)
@@ -491,7 +508,7 @@
         cot_ref[:, sixteen(index), :] = jnp.concatenate(both, 1).astype(BF)
         return carry
 
-    lax.fori_loop(0, 8, last, 0)
+    lax.fori_loop(0, 8, last, 0, unroll=2)
     store_back = pltpu.make_async_copy(cot_ref, back_hbm, store_sem.at[2])
     store_back.start()
     sent(s1, 2)
@@ -540,7 +557,7 @@
         out_specs=[AWAY, AWAY, AWAY, WHOLE, WHOLE],
         scratch_shapes=[
             block, block, pltpu.VMEM((2, C, C, 256), BF), grid, turned, turned, turned,
-            pltpu.VMEM((N * N, 256), F32), planes, planes, pltpu.VMEM((256 * 64, 128), F32),
+            pltpu.VMEM((N * N, 256), F32), planes, planes, pltpu.VMEM((256 * PITCH, 128), F32),
             modes, modes, modes, pltpu.VMEM((256, 256), BF),
             pltpu.VMEM((256, 256), F32), pltpu.VMEM((8, 256), F32),
             small(16), small(16), pltpu.VMEM((8, 128), F32), small(8), small(16),

time: 122 us -> 96.2 us (0.79)
  Pallas kernels: 110 us -> 84.7 us
    pallas_call x1, Pallas kernels: 110 us -> 84.7 us  [shards(): pl.pallas_call(layer, out_shape=(shape((C, 128, 128), BF), shape((C, 128,...]
where the time goes in v4:
time: 96.2 us; the launch traced here: 96.1 us
  Pallas kernels  84.7 us (88%)
  local copies, waits for them, and re-layouts  10.7 us (11%)
    pallas_call x1, Pallas kernels, shards(): pl.pallas_call(layer, out_shape=(shape((C, 128, 128), BF), shape((C, 128,...  84.7 us
    unnamed x13, local copies, waits for them, and re-layouts  10.7 us

profile of v4, /device:TPU:1, one launch (start us, length us, event | category | flops | bytes accessed | tf_op | source)
XLA Modules:
  0.0 96.1 jit_solution(5594579343237778124)
XLA Ops:
  0.6 84.7 %layer.1 = (bf16[64,128,128]{2,1,0:T(8,128)(2,1)}, bf16[64,128,128]{2,1,0:T(8,128)(2,1)}, bf16[2,64,64,256]{3,2,1,0:T(8,128)(2,1)}, f32[64,64]{1,0:T(8,128)}, f32[1,64]{1,0:T(1,128)}) custom-call(bf16[64,128,128]{2,1,0:T(8,128)(2,1)} %bitcast.22, bf16[64,128,128]{2,1,0:T(8,128)(2,1)} %bitcast.23, bf16[2,64,64,256]{3,2,1,0:T(8,128)(2,1)} %raw_hbm.1, ...), custom_call_target="tpu_custom_call" | custom-call | tf_op jit(solution)/shard_map/layer/pallas_call | solution.py:547
  85.3 0.0 copy-start.1
  85.4 4.6 %copy.29 = bf16[1,64,4,4096]{3,2,1,0:T(4,128)(2,1)} copy(bf16[1,64,4,4096]{3,2,1,0:T(4,128)(2,1)} %bitcast.25) | data formatting | bytes 4194304
  90.0 0.0 copy-done.1
  90.0 0.0 copy-start
  90.0 1.3 %copy.30 = bf16[1,64,4,4096]{3,2,1,0:T(4,128)(2,1)} copy(bf16[1,64,4,4096]{3,2,1,0:T(4,128)(2,1)S(1)} %bitcast.24) | data formatting | bytes 4194304
  91.3 1.6 %copy-done = bf16[2,64,64,256]{3,2,1,0:T(8,128)(2,1)S(1)} copy-done((bf16[2,64,64,256]{3,2,1,0:T(8,128)(2,1)S(1)}, bf16[2,64,64,256]{3,2,1,0:T(8,128)(2,1)}, u32[]{:S(2)}) %copy-start) | copy-done | bytes 4194328
  92.9 0.0 copy-start.2
  92.9 0.0 copy-start.3
  92.9 2.0 %copy.31 = bf16[2,64,64,256]{3,2,1,0:T(8,128)(2,1)} copy(bf16[2,64,64,256]{3,2,1,0:T(8,128)(2,1)S(1)} %copy-done) | data formatting | bytes 8388608
  94.9 0.0 copy-done.2
  94.9 0.6 copy.32
  95.6 0.0 copy-done.3
  95.6 0.5 copy.33
Async XLA Ops:
  85.3 4.6 %copy-start.1 = (bf16[64,128,128]{2,1,0:T(8,128)(2,1)S(1)}, bf16[64,128,128]{2,1,0:T(8,128)(2,1)}, u32[]{:S(2)}) copy-start(bf16[64,128,128]{2,1,0:T(8,128)(2,1)} %get-tuple-element.11) | copy-start | bytes 6291460
  90.0 2.9 %copy-start = (bf16[2,64,64,256]{3,2,1,0:T(8,128)(2,1)S(1)}, bf16[2,64,64,256]{3,2,1,0:T(8,128)(2,1)}, u32[]{:S(2)}) copy-start(bf16[2,64,64,256]{3,2,1,0:T(8,128)(2,1)} %get-tuple-element.22) | copy-start | bytes 12582916
  92.9 2.0 %copy-start.2 = (f32[64,64]{1,0:T(8,128)S(1)}, f32[64,64]{1,0:T(8,128)}, u32[]{:S(2)}) copy-start(f32[64,64]{1,0:T(8,128)} %get-tuple-element.23) | copy-start | bytes 49156
  92.9 2.6 %copy-start.3 = (f32[1,64]{1,0:T(1,128)S(1)}, f32[1,64]{1,0:T(1,128)}, u32[]{:S(2)}) copy-start(f32[1,64]{1,0:T(1,128)} %get-tuple-element.14) | copy-start | bytes 772

commit v5 on v4

--- a/solution.py
+++ b/solution.py
@@ -171,8 +171,7 @@
     row_mode = lax.broadcasted_iota(jnp.int32, (32, 128), 0) // 8
     low = low_lanes((32, 128))
 
-    def one(group, carry):
-        x = x_ref[pl.ds(pl.multiple_of(group * 32, 32), 32), :]
+    def spaced(x):
         xs = swap(x)
         zero = jnp.zeros_like(x)
         top, bottom = [], []
@@ -181,37 +180,47 @@
             odd = jnp.logical_and(row_mode == 2 * h + 1, jnp.logical_not(low))
             top.append(jnp.where(even, x, jnp.where(odd, xs, zero)))
             bottom.append(jnp.where(even, xs, jnp.where(odd, x, zero)))
-        left = jnp.concatenate(
-            [jnp.concatenate(top, 1), jnp.concatenate(bottom, 1)], 0
-        ).astype(BF)
-        w = four_rows(w_ref, group)
+        return [jnp.concatenate(top, 1), jnp.concatenate(bottom, 1)]
+
+    def one(group, carry):
+        rows = [pl.ds(pl.multiple_of(group * 64 + 32 * j, 32), 32) for j in range(2)]
+        left = jnp.concatenate(spaced(x_ref[rows[0], :]) + spaced(x_ref[rows[1], :]), 0).astype(BF)
+        w = jnp.concatenate([four_rows(w_ref, 2 * group), four_rows(w_ref, 2 * group + 1)], 1)
         z = dot(left, w)
-        p_ref[pl.ds(pl.multiple_of(group * 32, 32), 32), :] = z[:32] + signed_swap(z[32:], -1)
-        return carry
-
-    lax.fori_loop(32 * half, 32 * half + 32, one, 0, unroll=4)
+        for j in range(2):
+            y = z[64 * j : 64 * j + 64, 128 * j : 128 * j + 128]
+            p_ref[rows[j], :] = y[:32] + signed_swap(y[32:], -1)
+        return carry
+
+    lax.fori_loop(16 * half, 16 * half + 16, one, 0, unroll=4)
 
 
 def mix_back(g_ref, w_ref, p_ref, half):
     row_mode = lax.broadcasted_iota(jnp.int32, (32, 128), 0) // 8
     low = low_lanes((32, 128))
+    even = row_mode % 2 == 0
+    first = row_mode < 2
 
     def one(group, carry):
-        g = g_ref[pl.ds(pl.multiple_of(group * 32, 32), 32), :]
-        left = jnp.concatenate([g, signed_swap(g, 1)], 0).astype(BF)
-        w = four_rows(w_ref, group)
-        z = dot_nt(left, w)
-        z0, z1 = z[:32], z[32:]
-        even = row_mode % 2 == 0
-        first = row_mode < 2
-        a0 = jnp.where(first, z0[:, :128], z0[:, 128:])
-        a1 = jnp.where(first, z1[:, :128], z1[:, 128:])
-        b0 = jnp.where(even, a0, swap(a0))
-        b1 = jnp.where(even, swap(a1), a1)
-        p_ref[pl.ds(pl.multiple_of(group * 32, 32), 32), :] = jnp.where(low, b0, b1)
-        return carry
-
-    lax.fori_loop(32 * half, 32 * half + 32, one, 0, unroll=4)
+        rows = [pl.ds(pl.multiple_of(group * 64 + 32 * j, 32), 32) for j in range(2)]
+        left = []
+        for j in range(2):
+            g = g_ref[rows[j], :]
+            both = jnp.concatenate([g, signed_swap(g, 1)], 0)
+            none = jnp.zeros_like(both)
+            left.append(jnp.concatenate([both, none] if j == 0 else [none, both], 1))
+        w = jnp.concatenate([four_rows(w_ref, 2 * group), four_rows(w_ref, 2 * group + 1)], 1)
+        z = dot_nt(jnp.concatenate(left, 0).astype(BF), w)
+        for j in range(2):
+            z0, z1 = z[64 * j : 64 * j + 32], z[64 * j + 32 : 64 * j + 64]
+            a0 = jnp.where(first, z0[:, :128], z0[:, 128:])
+            a1 = jnp.where(first, z1[:, :128], z1[:, 128:])
+            b0 = jnp.where(even, a0, swap(a0))
+            b1 = jnp.where(even, swap(a1), a1)
+            p_ref[rows[j], :] = jnp.where(low, b0, b1)
+        return carry
+
+    lax.fori_loop(16 * half, 16 * half + 16, one, 0, unroll=4)
 
 
 ROOT = math.sqrt(2.0 / math.pi)
@@ -260,14 +269,23 @@
     lax.fori_loop(0, 64, turn, 0, unroll=4)
 
 
+def spread_map(skip_in, repeat_ref, kron_ref):
+    wide = dot_nt(dot(repeat_ref[...], skip_in[...]).astype(BF), repeat_ref[...])
+    same = (
+        lax.broadcasted_iota(jnp.int32, (256, 256), 0) // 64
+        == lax.broadcasted_iota(jnp.int32, (256, 256), 1) // 64
+    )
+    kron_ref[...] = jnp.where(same, wide, 0.0).astype(BF)
+
+
 def layer(
     field_hbm, cot_hbm, raw_hbm, skip_in, bias_in,
     d1_ref, d1t_ref, d2_ref, d2t_ref, fwd_ref, inv_ref, eye_ref, order_ref, back_order_ref, repeat_ref,
-    out_hbm, back_hbm, sg_hbm, skip_ref, line_ref,
+    out_hbm, sg_hbm, g_hbm, r4, skip_ref, line_ref,
     io_ref, cot_ref, raw_ref, v_ref, ct_ref, out_ref, g_ref, vk_ref, h_ref, b_ref, w_ref,
     x_ref, y_ref, p_ref, kron_ref,
     acc_ref, sum_ref, part_ref, slab_ref, half_ref, dp_ref, total_ref,
-    s1, s2, r1, r2, r3, r4,
+    s1, s2, r1, r2, r3,
     send_sem, recv_sem, local_sem, load_sem, store_sem, small_send, small_recv,
 ):
     dp = lax.axis_index("dp")
@@ -333,12 +351,7 @@
         for half in range(2):
             wait_bytes(s_ref.at[half, rest], send_sem.at[2 * phase + half])
 
-    wide = dot_nt(dot(repeat_ref[...], skip_in[...]).astype(BF), repeat_ref[...])
-    same = (
-        lax.broadcasted_iota(jnp.int32, (256, 256), 0) // 64
-        == lax.broadcasted_iota(jnp.int32, (256, 256), 1) // 64
-    )
-    kron_ref[...] = jnp.where(same, wide, 0.0).astype(BF)
+    spread_map(skip_in, repeat_ref, kron_ref)
     bias = jnp.concatenate([bias_in[...]] * 4, 1)
 
     load_field.wait()
@@ -405,6 +418,9 @@
     for half in range(2):
         stage_y(b_ref, d2_ref, s1, half)
         send(s1, r3, 2, half)
+
+    store_g = pltpu.make_async_copy(g_ref, g_hbm, store_sem.at[2])
+    store_g.start()
 
     acc_ref[...] = jnp.zeros_like(acc_ref)
     sum_ref[...] = jnp.zeros_like(sum_ref)
@@ -452,12 +468,6 @@
     store_out = pltpu.make_async_copy(io_ref, out_hbm, store_sem.at[0])
     store_out.start()
 
-    def skip_back(quad, carry):
-        vk_ref[columns(quad), :] = dot_nt(g_ref[columns(quad), :], kron_ref[...])
-        return carry
-
-    lax.fori_loop(0, 16, skip_back, 0, unroll=2)
-
     sent(s2, 1)
     for half in range(2):
         arrived(s1, r3, 2, half)
@@ -495,22 +505,6 @@
     total_ref[slab] = part_ref[slab]
     along_slab(lambda place: part_ref.at[slab], total_ref, slab, 2)
 
-    for half in range(2):
-        arrived(s2, r4, 3, half)
-        unstage_y(r4, d2t_ref, h_ref, half)
-
-    def last(index, carry):
-        both = []
-        for j in range(2):
-            quad = 2 * index + j
-            value = dot(d1t_ref[...], load_quad(h_ref, quad)) + vk_ref[columns(quad), :]
-            both.append(rows_together(dot_nt(back_order_ref[...], value.astype(BF))))
-        cot_ref[:, sixteen(index), :] = jnp.concatenate(both, 1).astype(BF)
-        return carry
-
-    lax.fori_loop(0, 8, last, 0, unroll=2)
-    store_back = pltpu.make_async_copy(cot_ref, back_hbm, store_sem.at[2])
-    store_back.start()
     sent(s1, 2)
     sent(s2, 3)
     wait_bytes(part_ref.at[few], small_send.at[2])
@@ -519,7 +513,71 @@
     line_ref[...] = total_ref[8][:1, :64]
     store_out.wait()
     store_sg.wait()
-    store_back.wait()
+    store_g.wait()
+    for half in range(2):
+        arrived(s2, r4, 3, half)
+
+
+def finish(
+    skip_in, skip_part, line_part, repeat_ref, r_hbm, g_hbm, d1t_hbm, d2t_hbm, order_hbm, out_part, sg_part,
+    back_hbm, skip_ref, line_ref, out_hbm, sg_hbm,
+    r_ref, g_ref, d1t_ref, d2t_ref, back_order_ref, out_ref, sg_ref,
+    back_ref, h_ref, kron_ref, load_sem, copy_sem, store_sem,
+):
+    sources = (r_hbm, d2t_hbm, d1t_hbm, order_hbm, g_hbm, out_part, sg_part)
+    targets = (r_ref, d2t_ref, d1t_ref, back_order_ref, g_ref, out_ref, sg_ref)
+    loads = [
+        pltpu.make_async_copy(source, target, load_sem.at[i])
+        for i, (source, target) in enumerate(zip(sources, targets))
+    ]
+    for load in loads[:5]:
+        load.start()
+    skip_ref[...] = skip_part[...]
+    line_ref[...] = line_part[...]
+    spread_map(skip_in, repeat_ref, kron_ref)
+    loads[0].wait()
+    loads[1].wait()
+    for half in range(2):
+        unstage_y(r_ref, d2t_ref, h_ref, half)
+    for load in loads[2:5]:
+        load.wait()
+    for load in loads[5:]:
+        load.start()
+
+    def last(index, carry):
+        both = []
+        for j in range(2):
+            quad = 2 * index + j
+            value = dot(d1t_ref[...], load_quad(h_ref, quad)) + dot_nt(
+                g_ref[columns(quad), :], kron_ref[...]
+            )
+            both.append(rows_together(dot_nt(back_order_ref[...], value.astype(BF))))
+        back_ref[:, sixteen(index), :] = jnp.concatenate(both, 1).astype(BF)
+        return carry
+
+    def store_back(part):
+        rows = pl.ds(32 * part, 32)
+        return pltpu.make_async_copy(back_ref.at[:, rows], back_hbm.at[:, rows], store_sem.at[part])
+
+    lax.fori_loop(0, 2, last, 0, unroll=2)
+    store_back(0).start()
+    lax.fori_loop(2, 4, last, 0, unroll=2)
+    store_back(1).start()
+    moves = [
+        pltpu.make_async_copy(out_ref, out_hbm, copy_sem.at[0]),
+        pltpu.make_async_copy(sg_ref, sg_hbm, copy_sem.at[1]),
+    ]
+    for load, move in zip(loads[5:], moves):
+        load.wait()
+        move.start()
+    lax.fori_loop(4, 6, last, 0, unroll=2)
+    store_back(2).start()
+    lax.fori_loop(6, 8, last, 0, unroll=2)
+    store_back(3).start()
+    for move in moves:
+        move.wait()
+    for part in range(4):
+        store_back(part).wait()
 
 
 WHOLE = pl.BlockSpec(memory_space=pltpu.VMEM)
@@ -528,6 +586,7 @@
 
 def shards(field, cotangent, spectral, skip, bias):
     constants = tuple(jnp.asarray(a) for a in tables())
+    d1, d1t, d2, d2t, fwd, inv, eye, order, back_order, repeat = constants
     shape = lambda dims, dtype: jax.ShapeDtypeStruct(dims, dtype)
 
     def gather(a):
@@ -542,19 +601,19 @@
     planes = pltpu.VMEM((8, 512, 256), BF)
     modes = pltpu.VMEM((2048, 128), F32)
     chunks = pltpu.VMEM((2, DEVICES, 16, 128), BF)
+    square = pltpu.VMEM((256, 256), BF)
     small = lambda count: pltpu.VMEM((count, 8, 128), F32)
     dma = pltpu.SemaphoreType.DMA
-    out, back, spectral_grad, skip_grad, bias_grad = pl.pallas_call(
+    narrow = (shape((C, C), F32), shape((1, C), F32))
+    weights = shape((2, C, C, 256), BF)
+    cells = shape((C, 128, 128), BF)
+    out, spectral_grad, g, r4, skip_grad, bias_grad = pl.pallas_call(
         layer,
         out_shape=(
-            shape((C, 128, 128), BF),
-            shape((C, 128, 128), BF),
-            shape((2, C, C, 256), BF),
-            shape((C, C), F32),
-            shape((1, C), F32),
+            cells, weights, shape((N * N, 256), BF), shape((2, DEVICES, 16, 128), BF), *narrow
         ),
         in_specs=[AWAY, AWAY, AWAY] + [WHOLE] * 12,
-        out_specs=[AWAY, AWAY, AWAY, WHOLE, WHOLE],
+        out_specs=[AWAY] * 4 + [WHOLE] * 2,
         scratch_shapes=[
             block, block, pltpu.VMEM((2, C, C, 256), BF), grid, turned, turned, turned,
             pltpu.VMEM((N * N, 256), F32), planes, planes, pltpu.VMEM((256 * PITCH, 128), F32),
@@ -562,13 +621,26 @@
             pltpu.VMEM((256, 256), F32), pltpu.VMEM((8, 256), F32),
             small(16), small(16), pltpu.VMEM((8, 128), F32), small(8), small(16),
         ]
-        + [chunks] * 6
+        + [chunks] * 5
         + [dma((8,)), dma((8,)), dma((8,)), dma((3,)), dma((3,)), dma((3,)), dma((3,))],
         compiler_params=pltpu.CompilerParams(
             collective_id=1, has_side_effects=True, vmem_limit_bytes=VMEM_LIMIT
         ),
         name="layer",
     )(gather(field), gather(cotangent), spectral, skip, bias.reshape(1, C), *constants)
+    back, skip_grad, bias_grad, out, spectral_grad = pl.pallas_call(
+        finish,
+        out_shape=(cells, *narrow, cells, weights),
+        in_specs=[WHOLE] * 4 + [AWAY] * 7,
+        out_specs=[AWAY, WHOLE, WHOLE, AWAY, AWAY],
+        scratch_shapes=[
+            chunks, turned, square, pltpu.VMEM((512, 256), BF), square, block,
+            pltpu.VMEM((2, C, C, 256), BF), block, planes, square,
+            dma((7,)), dma((2,)), dma((4,)),
+        ],
+        compiler_params=pltpu.CompilerParams(vmem_limit_bytes=VMEM_LIMIT),
+        name="finish",
+    )(skip, skip_grad, bias_grad, repeat, r4, g, d1t, d2t, back_order, out, spectral_grad)
     return (spread(out), spread(back), spectral_grad, skip_grad, bias_grad[0])
 
 

time: 96.2 us -> 92.4 us (0.960)
  local copies, waits for them, and re-layouts: 10.7 us -> 0 us
  Pallas kernels: 84.7 us -> 91.4 us
    unnamed x13 -> x0, local copies, waits for them, and re-layouts: 10.7 us -> none
    pallas_call x1 -> x2, Pallas kernels: 84.7 us -> 91.4 us  [the longest x1 81.1 us: shards(): pl.pallas_call(layer, out_shape=(cells, weights, shape((N * N, 256), BF),...]
where the time goes in v5:
time: 92.4 us; the launch traced here: 92.2 us
  Pallas kernels  91.4 us (99%)
    pallas_call x1, Pallas kernels, shards(): pl.pallas_call(layer, out_shape=(cells, weights, shape((N * N, 256), BF),...  81.1 us
    pallas_call x1, Pallas kernels, shards(): pl.pallas_call(finish, out_shape=(cells, *narrow, cells, weights), in_spe...  10.3 us

profile of v5, /device:TPU:1, one launch (start us, length us, event | category | flops | bytes accessed | tf_op | source)
XLA Modules:
  0.0 92.2 jit_solution(9212424858200980122)
XLA Ops:
  0.6 81.1 %layer.1 = (bf16[64,128,128]{2,1,0:T(8,128)(2,1)}, bf16[2,64,64,256]{3,2,1,0:T(8,128)(2,1)}, bf16[4096,256]{1,0:T(8,128)(2,1)}, bf16[2,128,16,128]{3,2,1,0:T(8,1...) custom-call(bf16[64,128,128]{2,1,0:T(8,128)(2,1)} %bitcast.22, bf16[64,128,128]{2,1,0:T(8,128)(2,1)} %bitcast.23, ...), custom_call_target="tpu_custom_call" | custom-call | tf_op jit(solution)/shard_map/layer/pallas_call | solution.py:610
  81.7 10.3 %finish.1 = (bf16[64,128,128]{2,1,0:T(8,128)(2,1)}, f32[64,64]{1,0:T(8,128)}, f32[1,64]{1,0:T(1,128)}, bf16[64,128,128]{2,1,0:T(8,128)(2,1)}, bf16[2,64,64,256]{3,2,1,0:T(8,128)(2,1)}) custom-call(bf16[64,64]{1,0:T(8,128)(2,1)} %skip_in.3, f32[64,64]{1,0:T(8,128)} %get-tuple-element.16.skip_part, f32[1,64]{1,0:T(1,128)} %get-tuple-element.17.line_part, ...), custom_call_target="tpu_custom_call" | custom-call | tf_op jit(solution)/shard_map/finish/pallas_call | solution.py:631

commit v6 on v5

--- a/solution.py
+++ b/solution.py
@@ -373,8 +373,9 @@
     send(s1, r1, 0, 1)
     load_raw.wait()
 
+    turn_weights(raw_ref, eye_ref, w_ref, 0)
+    turn_weights(raw_ref, eye_ref, w_ref, 1)
     for half in range(2):
-        turn_weights(raw_ref, eye_ref, w_ref, half)
         arrived(s1, r1, 0, half)
         line_forward(r1, fwd_ref, x_ref, half)
         mix(x_ref, w_ref, p_ref, half)
@@ -413,7 +414,7 @@
             store_quad(b_ref, quad, dot(d1_ref[...], g))
         return carry
 
-    lax.fori_loop(0, 8, point, 0, unroll=2)
+    lax.fori_loop(0, 8, point, 0, unroll=4)
     sent(s1, 0)
     for half in range(2):
         stage_y(b_ref, d2_ref, s1, half)

time: 92.4 us -> 90.4 us (0.978)
  Pallas kernels: 91.4 us -> 89.4 us
    pallas_call x1, Pallas kernels: 81.1 us -> 79.1 us  [shards(): pl.pallas_call(layer, out_shape=(cells, weights, shape((N * N, 256), BF),...]
where the time goes in v6:
time: 90.4 us; the launch traced here: 90.2 us
  Pallas kernels  89.4 us (99%)
    pallas_call x1, Pallas kernels, shards(): pl.pallas_call(layer, out_shape=(cells, weights, shape((N * N, 256), BF),...  79.1 us
    pallas_call x1, Pallas kernels, shards(): pl.pallas_call(finish, out_shape=(cells, *narrow, cells, weights), in_spe...  10.3 us

profile of v6, /device:TPU:1, one launch (start us, length us, event | category | flops | bytes accessed | tf_op | source)
XLA Modules:
  0.0 90.2 jit_solution(4373520604420607422)
XLA Ops:
  0.6 79.1 %layer.1 = (bf16[64,128,128]{2,1,0:T(8,128)(2,1)}, bf16[2,64,64,256]{3,2,1,0:T(8,128)(2,1)}, bf16[4096,256]{1,0:T(8,128)(2,1)}, bf16[2,128,16,128]{3,2,1,0:T(8,1...) custom-call(bf16[64,128,128]{2,1,0:T(8,128)(2,1)} %bitcast.22, bf16[64,128,128]{2,1,0:T(8,128)(2,1)} %bitcast.23, ...), custom_call_target="tpu_custom_call" | custom-call | tf_op jit(solution)/shard_map/layer/pallas_call | solution.py:611
  79.8 10.3 %finish.1 = (bf16[64,128,128]{2,1,0:T(8,128)(2,1)}, f32[64,64]{1,0:T(8,128)}, f32[1,64]{1,0:T(1,128)}, bf16[64,128,128]{2,1,0:T(8,128)(2,1)}, bf16[2,64,64,256]{3,2,1,0:T(8,128)(2,1)}) custom-call(bf16[64,64]{1,0:T(8,128)(2,1)} %skip_in.3, f32[64,64]{1,0:T(8,128)} %get-tuple-element.16.skip_part, f32[1,64]{1,0:T(1,128)} %get-tuple-element.17.line_part, ...), custom_call_target="tpu_custom_call" | custom-call | tf_op jit(solution)/shard_map/finish/pallas_call | solution.py:632

commit v7 on v6

--- a/solution.py
+++ b/solution.py
@@ -192,7 +192,7 @@
             p_ref[rows[j], :] = y[:32] + signed_swap(y[32:], -1)
         return carry
 
-    lax.fori_loop(16 * half, 16 * half + 16, one, 0, unroll=4)
+    lax.fori_loop(16 * half, 16 * half + 16, one, 0, unroll=8)
 
 
 def mix_back(g_ref, w_ref, p_ref, half):
@@ -220,7 +220,7 @@
             p_ref[rows[j], :] = jnp.where(low, b0, b1)
         return carry
 
-    lax.fori_loop(16 * half, 16 * half + 16, one, 0, unroll=4)
+    lax.fori_loop(16 * half, 16 * half + 16, one, 0, unroll=8)
 
 
 ROOT = math.sqrt(2.0 / math.pi)
@@ -257,7 +257,7 @@
             a_ref[pl.ds(first + PITCH * m, 64), :] = value[64 * m : 64 * m + 64]
         return carry
 
-    lax.fori_loop(0, 16, one, 0)
+    lax.fori_loop(0, 16, one, 0, unroll=2)
 
     def turn(i, carry):
         value = a_ref[pl.ds(i, 256, stride=PITCH), :].astype(BF)

time: 90.4 us -> 89 us (0.985)
  Pallas kernels: 89.4 us -> 88 us
    pallas_call x1, Pallas kernels: 79.1 us -> 77.7 us  [shards(): pl.pallas_call(layer, out_shape=(cells, weights, shape((N * N, 256), BF),...]
where the time goes in v7:
time: 89 us; the launch traced here: 88.8 us
  Pallas kernels  88 us (99%)
    pallas_call x1, Pallas kernels, shards(): pl.pallas_call(layer, out_shape=(cells, weights, shape((N * N, 256), BF),...  77.7 us
    pallas_call x1, Pallas kernels, shards(): pl.pallas_call(finish, out_shape=(cells, *narrow, cells, weights), in_spe...  10.3 us

profile of v7, /device:TPU:1, one launch (start us, length us, event | category | flops | bytes accessed | tf_op | source)
XLA Modules:
  0.0 88.8 jit_solution(4270808469163775886)
XLA Ops:
  0.6 77.7 %layer.1 = (bf16[64,128,128]{2,1,0:T(8,128)(2,1)}, bf16[2,64,64,256]{3,2,1,0:T(8,128)(2,1)}, bf16[4096,256]{1,0:T(8,128)(2,1)}, bf16[2,128,16,128]{3,2,1,0:T(8,1...) custom-call(bf16[64,128,128]{2,1,0:T(8,128)(2,1)} %bitcast.22, bf16[64,128,128]{2,1,0:T(8,128)(2,1)} %bitcast.23, ...), custom_call_target="tpu_custom_call" | custom-call | tf_op jit(solution)/shard_map/layer/pallas_call | solution.py:611
  78.3 10.3 %finish.1 = (bf16[64,128,128]{2,1,0:T(8,128)(2,1)}, f32[64,64]{1,0:T(8,128)}, f32[1,64]{1,0:T(1,128)}, bf16[64,128,128]{2,1,0:T(8,128)(2,1)}, bf16[2,64,64,256]{3,2,1,0:T(8,128)(2,1)}) custom-call(bf16[64,64]{1,0:T(8,128)(2,1)} %skip_in.3, f32[64,64]{1,0:T(8,128)} %get-tuple-element.16.skip_part, f32[1,64]{1,0:T(1,128)} %get-tuple-element.17.line_part, ...), custom_call_target="tpu_custom_call" | custom-call | tf_op jit(solution)/shard_map/finish/pallas_call | solution.py:632
